TPU v7x, 128 devices: a whole 4x4x4 slice. The times are simulated.
128 devices in a mesh: gx: 16 (over z, y), gy: 8 (over x, core).
Axes of the slice: x: 4, y: 4, z: 4, core: 2. Of those that a mesh axis runs over, the one named last changes fastest.
Arguments:
- owner_list: int32 [128, 128], replicated, may hold values from 0 to 128, as said below
- ice_mask: int32 [14336, 256], P(('gx', 'gy')), may hold values 0 or 1
- velocity: float32 [14336, 2, 256], P(('gx', 'gy')), may hold values from -2 to 2
- stress: float32 [14336, 3, 256], P(('gx', 'gy')), may hold values from -2 to 2
- thickness: float32 [14336, 5, 256], P(('gx', 'gy')), may hold values from 0.3 to 1.5
- concentration: float32 [14336, 5, 256], P(('gx', 'gy')), may hold values from 0.19 to 0.2
- ocean_u: float32 [2048, 2048], P('gy', 'gx'), may hold values from -3 to 3
- ocean_v: float32 [2048, 2048], P('gy', 'gx'), may hold values from -3 to 3
- wind_x: float32 [2048, 2048], P('gy', 'gx'), may hold values from -3 to 3
- wind_y: float32 [2048, 2048], P('gy', 'gx'), may hold values from -3 to 3
- surface_temp: float32 [2048, 2048], P('gy', 'gx'), may hold values from -4 to 4
Outputs:
- velocity_out: float32 [14336, 2, 256], P(('gx', 'gy'))
- stress_out: float32 [14336, 3, 256], P(('gx', 'gy'))
- ocean_drag: float32 [2, 2048, 2048], P(None, 'gy', 'gx')
Inputs may be any that keep to these rules, and one draw needn't show every extreme that they name: owner_list[s, k] is the owning device (linear index over gx then gy) of block k of ocean tile s, or the device count if the block holds no ice. Every device owns exactly 112 blocks; no tile has more than 2 blocks owned by one device, and some tile has exactly 2 owned by some device.
All inputs are finite; a program needn't handle non-finite values. No bound on the sum of `ice_mask` on one device may be relied on, other than what follows from the above.
Results may differ from a plain program's by a relative error of at most 0.00002.
Values sent between devices are 32-bit elements; how exact they have to be, the bound alone decides.
No kernel may reach another device: no remote copies, remote signals or barrier semaphores. Data moves between devices by JAX's collectives and lax.ppermute only.
A program may use at most 128 MiB of HBM per device.

v0:
```python
import jax
import jax.numpy as jnp
from jax import lax
from jax.experimental import pallas as pl
from jax.experimental.pallas import tpu as pltpu
from jax.sharding import PartitionSpec as P

AXES = ("gx", "gy")
TILES = 128
SLOTS = 112
ROWS = 256
LANES = 128
BANDS = ROWS // 8
HALO = 16
SUBS = 8
FIELDS = 8
FINAL = 5
I14 = 1.0 / 1.4
F32 = jnp.float32
VMEM_BYTES = 24 * 1024 * 1024


def lane_ids(rows=8):
    return lax.broadcasted_iota(jnp.int32, (rows, LANES), 1)


def roll(x, shift):
    return pltpu.roll(x, shift % LANES, 1)


def swap_chunks(four):
    lane = lane_ids(four[0].shape[0])
    low = lane < 64
    a, b, c, d = four
    a, c = jnp.where(low, a, roll(c, 64)), jnp.where(low, roll(a, 64), c)
    b, d = jnp.where(low, b, roll(d, 64)), jnp.where(low, roll(b, 64), d)
    even = (lane & 32) == 0
    a, b = jnp.where(even, a, roll(b, 32)), jnp.where(even, roll(a, 96), b)
    c, d = jnp.where(even, c, roll(d, 32)), jnp.where(even, roll(c, 96), d)
    return [a, b, c, d]


def pack_ice_kernel(
    owner_ref, mask_ref, vel_ref, str_ref, thk_ref, con_ref, out_ref, starts_ref, pos_ref, blk, near, sem
):
    me = lax.axis_index("gx") * lax.axis_size("gy") + lax.axis_index("gy")
    first = lax.broadcasted_iota(jnp.int32, (TILES, TILES), 0)
    second = lax.broadcasted_iota(jnp.int32, (TILES, TILES), 1)
    before = jnp.where(first < second, 1.0, 0.0)
    ones = jnp.ones((8, TILES), F32)
    owned = jnp.where(owner_ref[...] == me, 1.0, 0.0)
    counts = lax.dot_general(ones, owned, (((1,), (1,)), ((), ())), preferred_element_type=F32)
    starts = jnp.dot(counts, before, preferred_element_type=F32)
    starts_ref[...] = starts.astype(jnp.int32)
    copy = pltpu.make_async_copy(starts_ref, near, sem)
    copy.start()

    mine = jnp.broadcast_to(owner_ref[pl.ds(me, 1), :], (TILES, TILES)).astype(F32)
    twin = jnp.where(mine.T == mine, before, 0.0)
    rank = jnp.dot(ones, twin, preferred_element_type=F32)
    mine = mine[:8]
    pos_ref[...] = jnp.where(mine < TILES, 2.0 * mine + rank, -1.0).astype(jnp.int32)

    def block(i):
        con = con_ref[i]
        mass = jnp.sum(thk_ref[i] * con, axis=0, keepdims=True)
        total = jnp.sum(con, axis=0, keepdims=True)
        strength = mass * jnp.exp(-20.0 * (1.0 - total))
        cover = mask_ref[pl.ds(i, 1), :].astype(F32)
        for h in range(2):
            cut = slice(h * LANES, (h + 1) * LANES)
            at = h * FIELDS
            blk[i, at : at + 2, :] = vel_ref[i, :, cut]
            blk[i, at + 2 : at + 5, :] = str_ref[i, :, cut]
            blk[i, at + 5 : at + 6, :] = strength[:, cut]
            blk[i, at + 6 : at + 7, :] = mass[:, cut]
            blk[i, at + 7 : at + 8, :] = cover[:, cut]

    def some(g, carry):
        for j in range(8):
            block(g * 8 + j)
        return carry

    lax.fori_loop(0, SLOTS // 8, some, 0)
    copy.wait()
    for t in range(TILES):
        start = near[0, t]
        out_ref[2 * t] = blk[start]
        out_ref[2 * t + 1] = blk[start + 1]


def pack_ice(owner_list, ice_mask, velocity, stress, thickness, concentration):
    return pl.pallas_call(
        pack_ice_kernel,
        out_shape=(
            jax.ShapeDtypeStruct((2 * TILES, 2 * FIELDS, LANES), F32),
            jax.ShapeDtypeStruct((8, TILES), jnp.int32),
            jax.ShapeDtypeStruct((8, TILES), jnp.int32),
        ),
        scratch_shapes=[
            pltpu.VMEM((SLOTS + 8, 2 * FIELDS, LANES), F32),
            pltpu.SMEM((8, TILES), jnp.int32),
            pltpu.SemaphoreType.DMA(()),
        ],
        compiler_params=pltpu.CompilerParams(vmem_limit_bytes=VMEM_BYTES),
        name="pack_ice",
    )(owner_list, ice_mask, velocity, stress, thickness, concentration)


def ocean_edges_kernel(ou_ref, ov_ref, wx_ref, wy_ref, out_ref):
    lane = lane_ids()
    for i in range(BANDS):
        rows = slice(8 * i, 8 * i + 8)
        total = jnp.zeros((8, LANES), F32)
        for f, ref in enumerate((ou_ref, ov_ref, wx_ref, wy_ref)):
            x = ref[rows, :]
            total = jnp.where(lane // HALO == f, roll(x, f * HALO), total)
            total = jnp.where(lane // HALO == f + 4, roll(x, (f + 5) * HALO), total)
        out_ref[rows, :] = total


def ocean_edges(ou, ov, wx, wy):
    return pl.pallas_call(
        ocean_edges_kernel,
        out_shape=jax.ShapeDtypeStruct((ROWS, LANES), F32),
        name="ocean_edges",
    )(ou, ov, wx, wy)


def unpack_tile_kernel(pos_ref, recv_ref, temp_ref, tile_ref, west_ref, east_ref):
    lane = lane_ids()

    def band(i, carry):
        base = pl.multiple_of(i * 64, 64)
        row = pl.multiple_of(i * 8, 8)
        for h in range(2):
            four = []
            for c in range(4):
                pos = pos_ref[0, i * 4 + c]
                got = recv_ref[jnp.maximum(pos, 0), h * FIELDS : (h + 1) * FIELDS, :]
                four.append(jnp.where(pos >= 0, got, 0.0))
            for r, x in enumerate(swap_chunks(four)):
                tile_ref[pl.ds(base + h * 4 + r, FIELDS, stride=8), :] = x
        melt = jnp.exp(-0.5 * jnp.maximum(temp_ref[pl.ds(row, 8), :], 0.0))
        at = pl.multiple_of(base + 40, 8)
        tile_ref[pl.ds(at, 8), :] = tile_ref[pl.ds(at, 8), :] * melt
        west = jnp.zeros((8, LANES), F32)
        east = jnp.zeros((8, LANES), F32)
        for f in range(FIELDS):
            x = tile_ref[pl.ds(pl.multiple_of(base + f * 8, 8), 8), :]
            here = lane // HALO == f
            west = jnp.where(here, roll(x, f * HALO), west)
            east = jnp.where(here, roll(x, (f + 1) * HALO), east)
        west_ref[pl.ds(row, 8), :] = west
        east_ref[pl.ds(row, 8), :] = east
        return carry

    lax.fori_loop(0, BANDS, band, 0)


def unpack_tile(pos, recv, temp):
    return pl.pallas_call(
        unpack_tile_kernel,
        in_specs=[
            pl.BlockSpec(memory_space=pltpu.SMEM),
            pl.BlockSpec(memory_space=pltpu.VMEM),
            pl.BlockSpec(memory_space=pltpu.VMEM),
        ],
        out_shape=(
            jax.ShapeDtypeStruct((BANDS * FIELDS * 8, LANES), F32),
            jax.ShapeDtypeStruct((ROWS, LANES), F32),
            jax.ShapeDtypeStruct((ROWS, LANES), F32),
        ),
        compiler_params=pltpu.CompilerParams(vmem_limit_bytes=VMEM_BYTES),
        name="unpack_tile",
    )(pos, recv, temp)


STATE = ("u", "v", "p", "m", "t")
STATIC = ("ou", "ov", "wx", "wy", "inertia", "turn", "k", "cover")


def put_ice(s, i, ice, row_ids, grid_rows):
    u, v, total, diff, shear, strength, mass, cover = ice
    at = slice(8 + 8 * i, 16 + 8 * i)
    here = slice(8 * i, 8 * i + 8)
    s["u"][at, :] = u
    s["v"][at, :] = v
    s["p"][at, :] = cover * (total + diff)
    s["m"][at, :] = cover * (total - diff)
    s["t"][at, :] = cover * (shear + shear)
    coriolis = 2.0 * (row_ids.astype(F32) + 0.5) / grid_rows - 1.0
    s["inertia"][here, :] = 2.0 * mass
    s["turn"][here, :] = mass * coriolis
    s["k"][here, :] = (0.4 * I14) * (cover * strength)
    s["cover"][here, :] = cover


def put_ocean(s, i, ocean):
    here = slice(8 * i, 8 * i + 8)
    for name, x in zip(("ou", "ov", "wx", "wy"), ocean):
        s[name][here, :] = x


def clear_ends(s, chunks):
    zero = jnp.zeros((8, LANES), F32)
    for name in STATE:
        s[name][0:8, :] = zero
        s[name][8 + 8 * chunks : 16 + 8 * chunks, :] = zero


def run_subcycles(s, chunks):
    def subcycle(step, carry):
        for i in range(chunks):
            a = 8 + 8 * i
            at, up, down = slice(a, a + 8), slice(a + 1, a + 9), slice(a - 1, a + 7)
            here = slice(8 * i, 8 * i + 8)
            u, v = s["u"][at, :], s["v"][at, :]
            exx = roll(u, -1) - roll(u, 1)
            eyy = s["v"][up, :] - s["v"][down, :]
            shear = (s["u"][up, :] - s["u"][down, :]) + (roll(v, -1) - roll(v, 1))
            div = exx + eyy
            ten = exx - eyy
            q = div * div + 0.25 * (ten * ten + shear * shear) + 0.04
            inv = lax.rsqrt(q)
            k = s["k"][here, :] * inv
            base = div - q * inv
            ten = 0.25 * ten
            s["p"][at, :] = I14 * s["p"][at, :] + k * (base + ten)
            s["m"][at, :] = I14 * s["m"][at, :] + k * (base - ten)
            s["t"][at, :] = I14 * s["t"][at, :] + (0.25 * k) * shear
        for i in range(chunks):
            a = 8 + 8 * i
            at, up, down = slice(a, a + 8), slice(a + 1, a + 9), slice(a - 1, a + 7)
            here = slice(8 * i, 8 * i + 8)
            p, t = s["p"][at, :], s["t"][at, :]
            fx = 0.25 * ((roll(p, -1) - roll(p, 1)) + (s["t"][up, :] - s["t"][down, :]))
            fy = 0.25 * ((roll(t, -1) - roll(t, 1)) + (s["m"][up, :] - s["m"][down, :]))
            u, v = s["u"][at, :], s["v"][at, :]
            ou, ov = s["ou"][here, :], s["ov"][here, :]
            du, dv = ou - u, ov - v
            g = du * du + dv * dv + 0.01
            drag = g * lax.rsqrt(g)
            inertia, turn = s["inertia"][here, :], s["turn"][here, :]
            diag = inertia + drag
            rx = inertia * u + fx + s["wx"][here, :] + drag * ou
            ry = inertia * v + fy + s["wy"][here, :] + drag * ov
            w = s["cover"][here, :] / (diag * diag + turn * turn)
            s["u"][at, :] = w * (diag * rx + turn * ry)
            s["v"][at, :] = w * (diag * ry - turn * rx)
        return carry

    lax.fori_loop(0, SUBS, subcycle, 0)


def state_scratch(chunks):
    tall = pltpu.VMEM((8 * chunks + 16, LANES), F32)
    flat = pltpu.VMEM((8 * chunks, LANES), F32)
    return [tall] * len(STATE) + [flat] * len(STATIC)


def named(scratch):
    return dict(zip(STATE + STATIC, scratch))


def at_row(i):
    return lax.axis_index("gy") * ROWS + 8 * i + lax.broadcasted_iota(jnp.int32, (8, LANES), 0)


def chunk_of(tile_ref, i):
    return [tile_ref[i * 64 + f * 8 : i * 64 + f * 8 + 8, :] for f in range(FIELDS)]


def stresses(p, m, t):
    return 0.5 * (p + m), 0.5 * (p - m), 0.5 * t


def finals(s, i):
    at = slice(8 + 8 * i, 16 + 8 * i)
    return [s["u"][at, :], s["v"][at, :], *stresses(s["p"][at, :], s["m"][at, :], s["t"][at, :])]


def inner_kernel(tile_ref, ou_ref, ov_ref, wx_ref, wy_ref, out_ref, *scratch):
    s = named(scratch)
    grid_rows = ROWS * lax.axis_size("gy")
    clear_ends(s, BANDS)
    for i in range(BANDS):
        put_ice(s, i, chunk_of(tile_ref, i), at_row(i), grid_rows)
        put_ocean(s, i, [ref[8 * i : 8 * i + 8, :] for ref in (ou_ref, ov_ref, wx_ref, wy_ref)])
    run_subcycles(s, BANDS)
    for i in range(BANDS):
        for f, x in enumerate(finals(s, i)):
            out_ref[f, 8 * i : 8 * i + 8, :] = x


def inner(tile, ocean):
    return pl.pallas_call(
        inner_kernel,
        out_shape=jax.ShapeDtypeStruct((FINAL, ROWS, LANES), F32),
        scratch_shapes=state_scratch(BANDS),
        compiler_params=pltpu.CompilerParams(vmem_limit_bytes=VMEM_BYTES),
        cost_estimate=pl.CostEstimate(flops=4_000_000, bytes_accessed=4_000_000, transcendentals=800_000),
        name="inner",
    )(tile, *ocean)


def strip(own, west, east, lane):
    x = jnp.where(lane < 64, roll(own, HALO), roll(own, -HALO))
    x = jnp.where(lane < HALO, west, x)
    return jnp.where(lane >= LANES - HALO, east, x)


def ice_strips(own, west, east, edge, lane):
    west = jnp.where(edge[0], 0.0, west)
    east = jnp.where(edge[1], 0.0, east)
    return [
        strip(own[f], roll(west, -f * HALO), roll(east, LANES - HALO - f * HALO), lane) for f in range(FIELDS)
    ]


def ocean_strips(own, sides, lane):
    return [
        strip(own[f], roll(sides, -64 - f * HALO), roll(sides, LANES - HALO - f * HALO), lane) for f in range(4)
    ]


def edges_x():
    a = lax.axis_index("gx")
    return a == 0, a == lax.axis_size("gx") - 1


def edges_y():
    b = lax.axis_index("gy")
    return b == 0, b == lax.axis_size("gy") - 1


def join(mid, strips, lane):
    x = jnp.where(lane < HALO, roll(strips, -HALO), mid)
    return jnp.where(lane >= LANES - HALO, roll(strips, HALO), x)


def send_band(band, five, pos_ref, packed_ref, stage):
    for f, x in enumerate(five):
        for h in range(2):
            at = h * FINAL * 4 + f * 4
            stage[at : at + 4, :] = x[4 * h : 4 * h + 4, :]
    rows = [stage[pl.ds(r, 2 * FINAL, stride=4), :] for r in range(4)]
    for c, x in enumerate(swap_chunks(rows)):
        pos = pos_ref[0, band * 4 + c]

        @pl.when(pos >= 0)
        def _():
            packed_ref[pl.ds(pos * 2 * FINAL, 2 * FINAL), :] = x


def drag_rows(five, ou, ov, cover):
    du, dv = five[0] - ou, five[1] - ov
    g = du * du + dv * dv + 0.01
    drag = cover * (g * lax.rsqrt(g))
    return drag * du, drag * dv


def sides_kernel(
    pos_ref, tile_ref, west_ref, east_ref, sides_ref, ou_ref, ov_ref, wx_ref, wy_ref, mid_ref,
    packed_ref, drag_ref, stage, *scratch,
):
    s = named(scratch)
    lane = lane_ids()
    grid_rows = ROWS * lax.axis_size("gy")
    edge = edges_x()
    clear_ends(s, BANDS)
    for i in range(BANDS):
        rows = slice(8 * i, 8 * i + 8)
        ice = ice_strips(chunk_of(tile_ref, i), west_ref[rows, :], east_ref[rows, :], edge, lane)
        put_ice(s, i, ice, at_row(i), grid_rows)
        own = [ref[rows, :] for ref in (ou_ref, ov_ref, wx_ref, wy_ref)]
        put_ocean(s, i, ocean_strips(own, sides_ref[rows, :], lane))
    run_subcycles(s, BANDS)
    for i in range(2, BANDS - 2):
        rows = slice(8 * i, 8 * i + 8)
        five = [join(mid_ref[f, rows, :], x, lane) for f, x in enumerate(finals(s, i))]
        send_band(i, five, pos_ref, packed_ref, stage)
        cover = tile_ref[i * 64 + 56 : i * 64 + 64, :]
        drag_ref[0, rows, :], drag_ref[1, rows, :] = drag_rows(five, ou_ref[rows, :], ov_ref[rows, :], cover)


def specs(count):
    return [pl.BlockSpec(memory_space=pltpu.SMEM)] + [pl.BlockSpec(memory_space=pltpu.VMEM)] * (count - 1)


STAGE = pltpu.VMEM((2 * FINAL * 4, LANES), F32)
RESULTS = (
    jax.ShapeDtypeStruct((2 * TILES * 2 * FINAL, LANES), F32),
    jax.ShapeDtypeStruct((2, ROWS, LANES), F32),
)


def sides(pos, tile, west, east, ocean_sides, ocean, mid):
    return pl.pallas_call(
        sides_kernel,
        in_specs=specs(10),
        out_shape=RESULTS,
        scratch_shapes=[STAGE] + state_scratch(BANDS),
        compiler_params=pltpu.CompilerParams(vmem_limit_bytes=VMEM_BYTES),
        cost_estimate=pl.CostEstimate(flops=5_000_000, bytes_accessed=5_000_000, transcendentals=800_000),
        name="sides",
    )(pos, tile, west, east, ocean_sides, *ocean, mid)


def ends_kernel(
    pos_ref, tile_ref, west_ref, east_ref, north_ref, south_ref, sides_ref, osea_ref, nsea_ref,
    ou_ref, ov_ref, wx_ref, wy_ref, packed_in, drag_in, packed_ref, drag_ref, stage, *scratch,
):
    packed_ref[...] = packed_in[...]
    drag_ref[...] = drag_in[...]
    s = named(scratch)
    lane = lane_ids()
    grid_rows = ROWS * lax.axis_size("gy")
    edge = edges_x()
    outside = edges_y()
    ocean_refs = (ou_ref, ov_ref, wx_ref, wy_ref)
    clear_ends(s, 24)
    for end in range(2):
        ref, sea = ((north_ref, nsea_ref), (south_ref, osea_ref))[end]
        for j in range(6):
            i = (j - 2) if end == 0 else BANDS - 4 + j
            if 0 <= i < BANDS:
                rows = slice(8 * i, 8 * i + 8)
                own = chunk_of(tile_ref, i)
                west, east, near = west_ref[rows, :], east_ref[rows, :], sides_ref[rows, :]
                water = [x[rows, :] for x in ocean_refs]
            else:
                h = i % BANDS % 2
                own = [jnp.where(outside[end], 0.0, x) for x in chunk_of(ref, h)]
                west = jnp.where(outside[end], 0.0, ref[128 + 8 * h : 136 + 8 * h, :])
                east = jnp.where(outside[end], 0.0, ref[144 + 8 * h : 152 + 8 * h, :])
                near = sea[64 + 8 * h : 72 + 8 * h, :]
                water = [sea[16 * f + 8 * h : 16 * f + 8 * h + 8, :] for f in range(4)]
            for part in range(2):
                chunk = part * 12 + end * 6 + j
                put_ice(
                    s, chunk, ice_strips(own, west, east, edge, lane) if part else own, at_row(i), grid_rows
                )
                put_ocean(s, chunk, ocean_strips(water, near, lane) if part else water)
    run_subcycles(s, 24)
    for end in range(2):
        for j in (2, 3):
            i = (j - 2) if end == 0 else BANDS - 4 + j
            rows = slice(8 * i, 8 * i + 8)
            chunk = end * 6 + j
            five = [join(x, y, lane) for x, y in zip(finals(s, chunk), finals(s, chunk + 12))]
            send_band(i, five, pos_ref, packed_ref, stage)
            cover = tile_ref[i * 64 + 56 : i * 64 + 64, :]
            drag_ref[0, rows, :], drag_ref[1, rows, :] = drag_rows(
                five, ou_ref[rows, :], ov_ref[rows, :], cover
            )


def ends(pos, tile, west, east, north, south, ocean_sides, ocean_south, ocean_north, ocean, packed, drag):
    return pl.pallas_call(
        ends_kernel,
        in_specs=specs(15),
        out_shape=RESULTS,
        scratch_shapes=[STAGE] + state_scratch(24),
        compiler_params=pltpu.CompilerParams(vmem_limit_bytes=VMEM_BYTES),
        name="ends",
    )(pos, tile, west, east, north, south, ocean_sides, ocean_south, ocean_north, *ocean, packed, drag)


def unpack_ice_kernel(starts_ref, recv_ref, vel_ref, str_ref, blk):
    for t in range(TILES):
        start = starts_ref[0, t]
        for c in range(2):
            at = (2 * t + c) * 2 * FINAL
            blk[start + c, 0 : 2 * FINAL, :] = recv_ref[at : at + 2 * FINAL, :]

    def some(g, carry):
        for j in range(8):
            i = g * 8 + j
            for h in range(2):
                cut = slice(h * LANES, (h + 1) * LANES)
                vel_ref[i, :, cut] = blk[i, h * FINAL : h * FINAL + 2, :]
                str_ref[i, :, cut] = blk[i, h * FINAL + 2 : h * FINAL + 5, :]
        return carry

    lax.fori_loop(0, SLOTS // 8, some, 0)


def unpack_ice(starts, recv):
    return pl.pallas_call(
        unpack_ice_kernel,
        in_specs=specs(2),
        out_shape=(
            jax.ShapeDtypeStruct((SLOTS, 2, 2 * LANES), F32),
            jax.ShapeDtypeStruct((SLOTS, 3, 2 * LANES), F32),
        ),
        scratch_shapes=[pltpu.VMEM((SLOTS + 8, 16, LANES), F32)],
        compiler_params=pltpu.CompilerParams(vmem_limit_bytes=VMEM_BYTES),
        name="unpack_ice",
    )(starts, recv)


def both_ways(axis, forward, backward):
    n = lax.axis_size(axis)
    return (
        lax.ppermute(forward, axis, [(i, (i + 1) % n) for i in range(n)]),
        lax.ppermute(backward, axis, [((i + 1) % n, i) for i in range(n)]),
    )


def on_device(
    owner_list, ice_mask, velocity, stress, thickness, concentration, ocean_u, ocean_v, wind_x, wind_y, surface_temp
):
    ocean = (ocean_u, ocean_v, wind_x, wind_y)
    outbound, starts, pos = pack_ice(owner_list, ice_mask, velocity, stress, thickness, concentration)
    arrived = lax.all_to_all(outbound, AXES, split_axis=0, concat_axis=0, tiled=True)

    rim = ocean_edges(*ocean)
    from_west, from_east = both_ways("gx", rim, rim)
    ocean_sides = jnp.where(lane_ids(ROWS) < 64, from_east, from_west)
    low = jnp.concatenate([x[:HALO] for x in ocean] + [ocean_sides[:HALO]], axis=0)
    high = jnp.concatenate([x[-HALO:] for x in ocean] + [ocean_sides[-HALO:]], axis=0)
    ocean_north, ocean_south = both_ways("gy", high, low)

    tile, west_edge, east_edge = unpack_tile(pos, arrived, surface_temp)
    west, east = both_ways("gx", east_edge, west_edge)
    mid = inner(tile, ocean)
    low = jnp.concatenate([tile[:128], west[:HALO], east[:HALO]], axis=0)
    high = jnp.concatenate([tile[-128:], west[-HALO:], east[-HALO:]], axis=0)
    north, south = both_ways("gy", high, low)
    packed, drag = sides(pos, tile, west, east, ocean_sides, ocean, mid)
    packed, drag = ends(
        pos, tile, west, east, north, south, ocean_sides, ocean_south, ocean_north, ocean, packed, drag
    )

    homeward = packed.reshape(2 * TILES, FINAL, 2, LANES)
    back = lax.all_to_all(homeward, AXES, split_axis=0, concat_axis=0, tiled=True)
    vel, strs = unpack_ice(starts, back.reshape(2 * TILES * 2 * FINAL, LANES))
    return vel, strs, drag


def solution(mesh):
    blocks = P(AXES, None, None)
    return jax.shard_map(
        on_device,
        mesh=mesh,
        in_specs=(P(), P(AXES, None)) + (blocks,) * 4 + (P("gy", "gx"),) * 5,
        out_specs=(blocks, blocks, P(None, "gy", "gx")),
        check_vma=False,
    )
```

profile of v0, /device:TPU:1, one launch (start us, length us, event | category | flops | bytes accessed | tf_op | source)
XLA Modules:
  0.0 124.0 jit_solution(13875690684359674858)
XLA Ops:
  0.6 1.3 %copy.14.str_ref = f32[112,3,256]{2,1,0:T(4,128)S(1)} copy(f32[112,3,256]{2,0,1:T(8,128)} %param.14) | data formatting | bytes 688128 | tf_op args[3]
  1.9 0.0 copy-start.5
  1.9 0.0 copy-start.7
  2.0 1.5 %copy.15.thk_ref = f32[112,5,256]{2,1,0:T(8,128)S(1)} copy(f32[112,5,256]{2,0,1:T(8,128)} %param.15) | data formatting | bytes 1146880 | tf_op args[4]
  3.4 0.4 copy.16.con_ref
  3.8 1.3 %pack_ice.1 = (f32[256,16,128]{2,1,0:T(8,128)S(1)}, s32[8,128]{1,0:T(8,128)S(1)}, s32[8,128]{1,0:T(8,128)S(1)}) custom-call(s32[128,128]{1,0:T(8,128)S(1)} %copy-done.8, s32[112,256]{1,0:T(8,128)S(1)} %copy-done.7, f32[112,2,256]{2,1,0:T(2,128)S(1)} %copy-done.5, f32[112,3,256]{2,1,0:T(4,128)S(1)} %copy.14.str_ref, f32[112,5,256]{2,1,0:T(8,128)S(1)} %copy.15.thk_ref, ...), custom_call_target="tpu_custom_call" | custom-call | tf_op jit(solution)/shard_map/pack_ice/pallas_call | solution.py:93
  5.2 1.4 %copy-done.4 = f32[256,16,128]{2,1,0:T(8,128)} copy-done((f32[256,16,128]{2,1,0:T(8,128)}, f32[256,16,128]{2,1,0:T(8,128)S(1)}, u32[]{:S(2)}) %copy-start.4) | copy-done | bytes 2097176
  6.6 11.5 %all-to-all-start = ((f32[256,16,128]{2,1,0:T(8,128)}), f32[256,16,128]{2,1,0:T(8,128)S(1)}, u32[]{:S(2)}, u32[]{:S(2)}) async-start(f32[256,16,128]{2,1,0:T(8,128)} %copy-done.4), calls=%async_computation | async-start | bytes 4194304 | tf_op jit(solution)/shard_map/all_to_all | solution.py:516
  18.1 2.0 %ocean_edges.1 = f32[256,128]{1,0:T(8,128)} custom-call(f32[256,128]{1,0:T(8,128)} %ou_ref.7, f32[256,128]{1,0:T(8,128)} %ov_ref.7, f32[256,128]{1,0:T(8,128)} %wx_ref.7, f32[256,128]{1,0:T(8,128)} %wy_ref.7), custom_call_target="tpu_custom_call" | custom-call | tf_op jit(solution)/shard_map/ocean_edges/pallas_call | solution.py:123
  20.1 1.4 %collective-permute-start.5 = (f32[256,128]{1,0:T(8,128)}, f32[256,128]{1,0:T(8,128)S(1)}, u32[]{:S(2)}, u32[]{:S(2)}) collective-permute-start(f32[256,128]{1,0:T(8,128)} %ocean_edges.1), channel_id=1, source_target_pairs={{0,8},{8,16},{16,24},{24,32},{32,40},{40,48},{48,56},{56,64},{64,7... | collective-permute-start | bytes 393224 | tf_op jit(solution)/shard_map/ppermute | solution.py:506
  21.5 4.2 %collective-permute-start.4 = (f32[256,128]{1,0:T(8,128)}, f32[256,128]{1,0:T(8,128)S(1)}, u32[]{:S(2)}, u32[]{:S(2)}) collective-permute-start(f32[256,128]{1,0:T(8,128)} %ocean_edges.1), channel_id=1, source_target_pairs={{8,0},{16,8},{24,16},{32,24},{40,32},{48,40},{56,48},{64,56},{72,6... | collective-permute-start | bytes 393224 | tf_op jit(solution)/shard_map/ppermute | solution.py:507
  25.8 23.1 %collective-permute-done.5 = f32[256,128]{1,0:T(8,128)S(1)} collective-permute-done((f32[256,128]{1,0:T(8,128)}, f32[256,128]{1,0:T(8,128)S(1)}, u32[]{:S(2)}, u32[]{:S(2)}) %collective-permute-start.5) | collective-permute-done | bytes 131104 | tf_op jit(solution)/shard_map/ppermute | solution.py:506
  48.9 8.3 %unpack_tile.1 = (f32[2048,128]{1,0:T(8,128)S(1)}, f32[256,128]{1,0:T(8,128)S(1)}, f32[256,128]{1,0:T(8,128)S(1)}) custom-call(s32[8,128]{1,0:T(8,128)S(1)} %get-tuple-element.16.pos_ref, f32[256,16,128]{2,1,0:T(8,128)S(1)} %all-to-all-done.recv_ref, f32[256,128]{1,0:T(8,128)S(1)} %copy-done.6), custom_call_target="tpu_custom_call" | custom-call | tf_op jit(solution)/shard_map/unpack_tile/pallas_call | solution.py:162
  57.2 0.1 collective-permute-start
  57.3 4.8 %collective-permute-start.1 = (f32[256,128]{1,0:T(8,128)S(1)}, f32[256,128]{1,0:T(8,128)S(1)}, u32[]{:S(2)}, u32[]{:S(2)}) collective-permute-start(f32[256,128]{1,0:T(8,128)S(1)} %get-tuple-element.20), channel_id=1, source_target_pairs={{8,0},{16,8},{24,16},{32,24},{40,32},{48,40},{56,48},{64,56},{72,6... | collective-permute-start | bytes 393224 | tf_op jit(solution)/shard_map/ppermute | solution.py:507
  62.1 2.3 %collective-permute-done.west_ref = f32[256,128]{1,0:T(8,128)S(1)} collective-permute-done((f32[256,128]{1,0:T(8,128)S(1)}, f32[256,128]{1,0:T(8,128)S(1)}, u32[]{:S(2)}, u32[]{:S(2)}) %collective-permute-start) | collective-permute-done | bytes 131104 | tf_op jit(solution)/shard_map/ppermute | solution.py:506
  64.4 3.7 %collective-permute-start.2 = (f32[160,128]{1,0:T(8,128)S(1)}, f32[160,128]{1,0:T(8,128)S(1)}, u32[]{:S(2)}, u32[]{:S(2)}) collective-permute-start(f32[160,128]{1,0:T(8,128)S(1)} %pad_maximum_fusion), channel_id=1, source_target_pairs={{0,1},{1,2},{2,3},{3,4},{4,5},{5,6},{6,7},{7,0},{8,9},{9,10},{10,1... | collective-permute-start | bytes 245768 | tf_op jit(solution)/shard_map/ppermute | solution.py:506
  68.1 1.7 %collective-permute-start.7 = (f32[80,128]{1,0:T(8,128)S(1)}, f32[80,128]{1,0:T(8,128)S(1)}, u32[]{:S(2)}, u32[]{:S(2)}) collective-permute-start(f32[80,128]{1,0:T(8,128)S(1)} %get-tuple-element.32), channel_id=1, source_target_pairs={{0,1},{1,2},{2,3},{3,4},{4,5},{5,6},{6,7},{7,0},{8,9},{9,10},{10,1... | collective-permute-start | bytes 122888 | tf_op jit(solution)/shard_map/ppermute | solution.py:506
  69.9 3.3 %inner.1.mid_ref = f32[5,256,128]{2,1,0:T(8,128)S(1)} custom-call(f32[2048,128]{1,0:T(8,128)S(1)} %get-tuple-element.18.tile_ref, f32[256,128]{1,0:T(8,128)S(1)} %copy-done, f32[256,128]{1,0:T(8,128)S(1)} %copy-done.1, f32[256,128]{1,0:T(8,128)S(1)} %copy-done.2, f32[256,128]{1,0:T(8,128)S(1)} %copy-done.3), custom_call_target="tpu_custom_call" | custom-call | flops 4000000 | bytes 4000000 | tf_op jit(solution)/shard_map/inner/pallas_call | solution.py:297
  73.2 11.9 %sides.1 = (f32[2560,128]{1,0:T(8,128)S(1)}, f32[2,256,128]{2,1,0:T(8,128)S(1)}) custom-call(s32[8,128]{1,0:T(8,128)S(1)} %get-tuple-element.16.pos_ref, f32[2048,128]{1,0:T(8,128)S(1)} %get-tuple-element.18.tile_ref, f32[256,128]{1,0:T(8,128)S(1)} %collective-permute-done.west_ref, f32[256,128]{1,0:T(8,128)S(1)} %collective-permute-done.1.east_ref, ...), custom_call_target="tpu_custom_call" | custom-call | flops 5000000 | bytes 5000000 | tf_op jit(solution)/shard_map/sides/pallas_call | solution.py:399
  85.1 5.4 %ends.1 = (f32[2560,128]{1,0:T(8,128)S(1)}, f32[2,256,128]{2,1,0:T(8,128)}) custom-call(s32[8,128]{1,0:T(8,128)S(1)} %get-tuple-element.16.pos_ref, f32[2048,128]{1,0:T(8,128)S(1)} %get-tuple-element.18.tile_ref, f32[256,128]{1,0:T(8,128)S(1)} %collective-permute-done.west_ref, f32[256,128]{1,0:T(8,128)S(1)} %collective-permute-done.1.east_ref, ...), custom_call_target="tpu_custom_call" | custom-call | tf_op jit(solution)/shard_map/ends/pallas_call | solution.py:460
  90.5 31.0 %all_to_all.10 = f32[256,5,2,128]{3,2,1,0:T(2,128)S(1)} all-to-all(f32[256,5,2,128]{3,2,1,0:T(2,128)S(1)} %bitcast.3), channel_id=1, replica_groups=mesh['gx'=16,'gy'=8] {'gx','gy'}, dimensions={0} | all-to-all | bytes 2621440 | tf_op jit(solution)/shard_map/all_to_all | solution.py:537
  121.6 1.7 %unpack_ice.1 = (f32[112,2,256]{2,1,0:T(2,128)}, f32[112,3,256]{2,1,0:T(4,128)S(1)}) custom-call(s32[8,128]{1,0:T(8,128)S(1)} %get-tuple-element.15.starts_ref, f32[2560,128]{1,0:T(8,128)S(1)} %bitcast.2), custom_call_target="tpu_custom_call" | custom-call | tf_op jit(solution)/shard_map/unpack_ice/pallas_call | solution.py:490
  123.2 0.8 copy.17
  (38 shorter events, 0.1 us)
Async XLA Ops:
  0.6 2.8 %copy-start.9 = (f32[112,5,256]{2,0,1:T(8,128)S(1)}, f32[112,5,256]{2,0,1:T(8,128)}, u32[]{:S(2)}) copy-start(f32[112,5,256]{2,0,1:T(8,128)} %param.16) | copy-start | bytes 1720324
  1.9 1.9 %copy-start.5 = (f32[112,2,256]{2,1,0:T(2,128)S(1)}, f32[112,2,256]{2,1,0:T(2,128)}, u32[]{:S(2)}) copy-start(f32[112,2,256]{2,1,0:T(2,128)} %vel_ref.1) | copy-start | bytes 688132
  1.9 1.9 %copy-start.7 = (s32[112,256]{1,0:T(8,128)S(1)}, s32[112,256]{1,0:T(8,128)}, u32[]{:S(2)}) copy-start(s32[112,256]{1,0:T(8,128)} %mask_ref.1) | copy-start | bytes 344068
  1.9 1.9 %copy-start.8 = (s32[128,128]{1,0:T(8,128)S(1)}, s32[128,128]{1,0:T(8,128)}, u32[]{:S(2)}) copy-start(s32[128,128]{1,0:T(8,128)} %owner_ref.1) | copy-start | bytes 196612
  5.2 1.4 %copy-start.4 = (f32[256,16,128]{2,1,0:T(8,128)}, f32[256,16,128]{2,1,0:T(8,128)S(1)}, u32[]{:S(2)}) copy-start(f32[256,16,128]{2,1,0:T(8,128)S(1)} %get-tuple-element.17) | copy-start | bytes 6291460
  6.5 19.1 %copy-start = (f32[256,128]{1,0:T(8,128)S(1)}, f32[256,128]{1,0:T(8,128)}, u32[]{:S(2)}) copy-start(f32[256,128]{1,0:T(8,128)} %ou_ref.7) | copy-start | bytes 393220
  6.6 19.1 %copy-start.1 = (f32[256,128]{1,0:T(8,128)S(1)}, f32[256,128]{1,0:T(8,128)}, u32[]{:S(2)}) copy-start(f32[256,128]{1,0:T(8,128)} %ov_ref.7) | copy-start | bytes 393220
  6.6 19.1 %copy-start.2 = (f32[256,128]{1,0:T(8,128)S(1)}, f32[256,128]{1,0:T(8,128)}, u32[]{:S(2)}) copy-start(f32[256,128]{1,0:T(8,128)} %wx_ref.7) | copy-start | bytes 393220
  6.6 19.2 %copy-start.3 = (f32[256,128]{1,0:T(8,128)S(1)}, f32[256,128]{1,0:T(8,128)}, u32[]{:S(2)}) copy-start(f32[256,128]{1,0:T(8,128)} %wy_ref.7) | copy-start | bytes 393220
  6.6 42.3 %copy-start.6 = (f32[256,128]{1,0:T(8,128)S(1)}, f32[256,128]{1,0:T(8,128)}, u32[]{:S(2)}) copy-start(f32[256,128]{1,0:T(8,128)} %temp_ref.1) | copy-start | bytes 393220
  6.6 42.3 %all-to-all-start = ((f32[256,16,128]{2,1,0:T(8,128)}), f32[256,16,128]{2,1,0:T(8,128)S(1)}, u32[]{:S(2)}, u32[]{:S(2)}) async-start(f32[256,16,128]{2,1,0:T(8,128)} %copy-done.4), calls=%async_computation | async-start | bytes 4194304 | tf_op jit(solution)/shard_map/all_to_all | solution.py:516
  20.1 28.8 %collective-permute-start.5 = (f32[256,128]{1,0:T(8,128)}, f32[256,128]{1,0:T(8,128)S(1)}, u32[]{:S(2)}, u32[]{:S(2)}) collective-permute-start(f32[256,128]{1,0:T(8,128)} %ocean_edges.1), channel_id=1, source_target_pairs={{0,8},{8,16},{16,24},{24,32},{32,40},{40,48},{48,56},{56,64},{64,7... | collective-permute-start | bytes 393224 | tf_op jit(solution)/shard_map/ppermute | solution.py:506
  21.5 27.4 %collective-permute-start.4 = (f32[256,128]{1,0:T(8,128)}, f32[256,128]{1,0:T(8,128)S(1)}, u32[]{:S(2)}, u32[]{:S(2)}) collective-permute-start(f32[256,128]{1,0:T(8,128)} %ocean_edges.1), channel_id=1, source_target_pairs={{8,0},{16,8},{24,16},{32,24},{40,32},{48,40},{56,48},{64,56},{72,6... | collective-permute-start | bytes 393224 | tf_op jit(solution)/shard_map/ppermute | solution.py:507
  57.2 7.2 %collective-permute-start = (f32[256,128]{1,0:T(8,128)S(1)}, f32[256,128]{1,0:T(8,128)S(1)}, u32[]{:S(2)}, u32[]{:S(2)}) collective-permute-start(f32[256,128]{1,0:T(8,128)S(1)} %get-tuple-element.19), channel_id=1, source_target_pairs={{0,8},{8,16},{16,24},{24,32},{32,40},{40,48},{48,56},{56,64},{64,7... | collective-permute-start | bytes 393224 | tf_op jit(solution)/shard_map/ppermute | solution.py:506
  57.3 7.1 %collective-permute-start.1 = (f32[256,128]{1,0:T(8,128)S(1)}, f32[256,128]{1,0:T(8,128)S(1)}, u32[]{:S(2)}, u32[]{:S(2)}) collective-permute-start(f32[256,128]{1,0:T(8,128)S(1)} %get-tuple-element.20), channel_id=1, source_target_pairs={{8,0},{16,8},{24,16},{32,24},{40,32},{48,40},{56,48},{64,56},{72,6... | collective-permute-start | bytes 393224 | tf_op jit(solution)/shard_map/ppermute | solution.py:507
  64.4 20.7 %collective-permute-start.2 = (f32[160,128]{1,0:T(8,128)S(1)}, f32[160,128]{1,0:T(8,128)S(1)}, u32[]{:S(2)}, u32[]{:S(2)}) collective-permute-start(f32[160,128]{1,0:T(8,128)S(1)} %pad_maximum_fusion), channel_id=1, source_target_pairs={{0,1},{1,2},{2,3},{3,4},{4,5},{5,6},{6,7},{7,0},{8,9},{9,10},{10,1... | collective-permute-start | bytes 245768 | tf_op jit(solution)/shard_map/ppermute | solution.py:506
  68.1 17.0 %collective-permute-start.3 = (f32[160,128]{1,0:T(8,128)S(1)}, f32[160,128]{1,0:T(8,128)S(1)}, u32[]{:S(2)}, u32[]{:S(2)}) collective-permute-start(f32[160,128]{1,0:T(8,128)S(1)} %pad_maximum_fusion.1), channel_id=1, source_target_pairs={{1,0},{2,1},{3,2},{4,3},{5,4},{6,5},{7,6},{0,7},{9,8},{10,9},{11,1... | collective-permute-start | bytes 245768 | tf_op jit(solution)/shard_map/ppermute | solution.py:507
  68.1 16.9 %collective-permute-start.7 = (f32[80,128]{1,0:T(8,128)S(1)}, f32[80,128]{1,0:T(8,128)S(1)}, u32[]{:S(2)}, u32[]{:S(2)}) collective-permute-start(f32[80,128]{1,0:T(8,128)S(1)} %get-tuple-element.32), channel_id=1, source_target_pairs={{0,1},{1,2},{2,3},{3,4},{4,5},{5,6},{6,7},{7,0},{8,9},{9,10},{10,1... | collective-permute-start | bytes 122888 | tf_op jit(solution)/shard_map/ppermute | solution.py:506
  69.9 15.2 %collective-permute-start.6 = (f32[80,128]{1,0:T(8,128)S(1)}, f32[80,128]{1,0:T(8,128)S(1)}, u32[]{:S(2)}, u32[]{:S(2)}) collective-permute-start(f32[80,128]{1,0:T(8,128)S(1)} %get-tuple-element.33), channel_id=1, source_target_pairs={{1,0},{2,1},{3,2},{4,3},{5,4},{6,5},{7,6},{0,7},{9,8},{10,9},{11,1... | collective-permute-start | bytes 122888 | tf_op jit(solution)/shard_map/ppermute | solution.py:507
where the time goes:
time: 124 us
  Pallas kernels  33.9 us (27%)
  blocking collectives  31 us (25%)
  starting transfers between devices  27.3 us (22%)
  waiting for transfers between devices  25.5 us (21%)
  local copies, waits for them, and re-layouts  5.32 us (4%)
    all_to_all x1, blocking collectives, on_device(): lax.all_to_all(homeward, AXES, split_axis=0, concat_axis=0, tiled=True)  31 us
    ppermute x4, waiting for transfers between devices, both_ways(): lax.ppermute(forward, axis, [(i, (i + 1) % n) for i in range(n)])  25.5 us
    pallas_call x1, Pallas kernels, sides(): pl.pallas_call(sides_kernel, in_specs=specs(10), out_shape=RESULTS, scrat...  11.9 us
    all_to_all x1, starting transfers between devices, on_device(): lax.all_to_all(outbound, AXES, split_axis=0, concat_axis=0, tiled=True)  11.5 us
    ppermute x4, starting transfers between devices, both_ways(): lax.ppermute(backward, axis, [((i + 1) % n, i) for i in range(n)])  8.96 us
    pallas_call x1, Pallas kernels, unpack_tile(): pl.pallas_call(unpack_tile_kernel, in_specs=[pl.BlockSpec(memory_space=pl...  8.28 us
    ppermute x4, starting transfers between devices, both_ways(): lax.ppermute(forward, axis, [(i, (i + 1) % n) for i in range(n)])  6.85 us
    pallas_call x1, Pallas kernels, ends(): pl.pallas_call(ends_kernel, in_specs=specs(15), out_shape=RESULTS, scratc...  5.4 us
  transfers between devices with their start and end apart: 9, of which 2 were waited for; matrix products, arithmetic and copies ran while one was open for 0% of the time, Pallas kernels for 14%

commit v1 on v0

v1 whole, which is shorter than its diff:
```python
import jax
import jax.numpy as jnp
from jax import lax
from jax.experimental import pallas as pl
from jax.experimental.pallas import tpu as pltpu
from jax.sharding import PartitionSpec as P

AXES = ("gx", "gy")
TILES = 128
SLOTS = 112
ROWS = 256
LANES = 128
BANDS = ROWS // 8
HALO = 16
SUBS = 8
FIELDS = 8
FINAL = 5
I14 = 1.0 / 1.4
F32 = jnp.float32
VMEM_BYTES = 24 * 1024 * 1024


def specs(count):
    return [pl.BlockSpec(memory_space=pltpu.SMEM)] + [pl.BlockSpec(memory_space=pltpu.VMEM)] * (count - 1)


def lane_ids(rows=8):
    return lax.broadcasted_iota(jnp.int32, (rows, LANES), 1)


def roll(x, shift):
    return pltpu.roll(x, shift % LANES, 1)


def interleave(tasks, width):
    tasks = list(tasks)
    active = []
    while tasks or active:
        if tasks and len(active) < width:
            active.append(tasks.pop(0))
        running = []
        for task in active:
            try:
                next(task)
                running.append(task)
            except StopIteration:
                pass
        active = running


def swap_chunks(quads):
    lane = lane_ids(quads[0][0].shape[0])
    low, even = lane < 64, (lane & 32) == 0
    far = [(roll(jnp.where(low, c, a), 64), roll(jnp.where(low, d, b), 64)) for a, b, c, d in quads]
    yield
    quads = [
        (jnp.where(low, a, ac), jnp.where(low, b, bd), jnp.where(low, ac, c), jnp.where(low, bd, d))
        for (a, b, c, d), (ac, bd) in zip(quads, far)
    ]
    near = [(roll(b, 32), roll(a, 96), roll(d, 32), roll(c, 96)) for a, b, c, d in quads]
    yield
    return [
        (jnp.where(even, a, p), jnp.where(even, q, b), jnp.where(even, c, r), jnp.where(even, t, d))
        for (a, b, c, d), (p, q, r, t) in zip(quads, near)
    ]


def pack_kernel(*refs):
    far, refs = refs[:11], refs[11:]
    (out_ref, starts_ref, pos_ref, west_ref, east_ref), refs = refs[:5], refs[5:]
    here, (blk, near, sem, sems) = refs[:11], refs[11:]
    ou_ref, ov_ref, wx_ref, wy_ref, _, owner_ref, con_ref, thk_ref, str_ref, mask_ref, vel_ref = here
    loads = [pltpu.make_async_copy(x, y, sems.at[n]) for n, (x, y) in enumerate(zip(far, here))]
    for n in (*range(5, 11), *range(5)):
        loads[n].start()
    loads[5].wait()
    me = lax.axis_index("gx") * lax.axis_size("gy") + lax.axis_index("gy")
    first = lax.broadcasted_iota(jnp.int32, (TILES, TILES), 0)
    second = lax.broadcasted_iota(jnp.int32, (TILES, TILES), 1)
    before = jnp.where(first < second, 1.0, 0.0)
    ones = jnp.ones((8, TILES), F32)
    owned = jnp.where(owner_ref[...] == me, 1.0, 0.0)
    counts = lax.dot_general(ones, owned, (((1,), (1,)), ((), ())), preferred_element_type=F32)
    starts = jnp.dot(counts, before, preferred_element_type=F32)
    starts_ref[...] = starts.astype(jnp.int32)
    copy = pltpu.make_async_copy(starts_ref, near, sem)
    copy.start()

    mine = jnp.broadcast_to(owner_ref[pl.ds(me, 1), :], (TILES, TILES)).astype(F32)
    column = mine.T
    rank = jnp.dot(ones, jnp.where(column == mine, before, 0.0), preferred_element_type=F32)
    per_owner = jnp.dot(ones, jnp.where(column == second.astype(F32), 1.0, 0.0), preferred_element_type=F32)
    lane = lane_ids().astype(F32)
    free = jnp.min(jnp.where(per_owner < 2.0, lane, 1000.0), axis=1, keepdims=True)
    mine = mine[:8]
    icy = mine < TILES
    slot = jnp.where(icy, 2.0 * mine + rank, 2.0 * free + 1.0)
    row = lax.broadcasted_iota(jnp.int32, (8, TILES), 0)
    pos_ref[...] = jnp.where(row == 0, slot, jnp.where(icy, 1.0, 0.0)).astype(jnp.int32)

    for n in range(6, 11):
        loads[n].wait()
    for g in range(SLOTS // 8):
        eight = slice(8 * g, 8 * g + 8)
        for h in range(2):
            cut = slice(h * LANES, (h + 1) * LANES)
            con = [con_ref[c, eight, cut] for c in range(5)]
            mass = sum(thk_ref[c, eight, cut] * con[c] for c in range(5))
            strength = mass * jnp.exp(-20.0 * (1.0 - sum(con)))
            rows = [str_ref[f, eight, cut] for f in range(3)]
            rows += [strength, mass, mask_ref[eight, cut].astype(F32)]
            for f, x in enumerate(rows):
                blk[pl.ds(128 * g + 8 * h + 2 + f, 8, stride=16), :] = x
            for j in range(8):
                at = 128 * g + 16 * j + 8 * h
                blk[at : at + 2, :] = vel_ref[8 * g + j, :, cut]

    for n in range(5):
        loads[n].wait()
    chunk = lane_ids() // HALO

    def sea_edges(i):
        moved = []
        for half in range(2):
            rows = slice(8 * i + half * LANES, 8 * i + half * LANES + 8)
            for f, ref in enumerate((ou_ref, ov_ref, wx_ref, wy_ref)):
                moved.append(roll(ref[rows, :], (4 * half + f) * HALO))
        yield
        west, east = moved[0], moved[0]
        for n in range(1, 8):
            west = jnp.where(chunk == n, moved[n], west)
            east = jnp.where(chunk == n - 1, moved[n], east)
        west_ref[8 * i : 8 * i + 8, :] = west
        east_ref[8 * i : 8 * i + 8, :] = east

    interleave([sea_edges(i) for i in range(BANDS // 2)], 5)

    copy.wait()
    for t in range(TILES):
        at = pl.multiple_of(near[0, t] * 16, 16)
        out_ref[2 * t] = blk[pl.ds(at, 16), :]
        out_ref[2 * t + 1] = blk[pl.ds(at + 16, 16), :]


def pack(owner_list, ice_mask, velocity, stress, thickness, concentration, maps):
    def by_field(x):
        return jnp.transpose(x, (1, 0, 2))

    inputs = (
        *maps, owner_list, by_field(concentration), by_field(thickness), by_field(stress), ice_mask, velocity
    )
    return pl.pallas_call(
        pack_kernel,
        in_specs=[pl.BlockSpec(memory_space=pltpu.HBM)] * 11,
        out_shape=(
            jax.ShapeDtypeStruct((2 * TILES, 2 * FIELDS, LANES), F32),
            jax.ShapeDtypeStruct((8, TILES), jnp.int32),
            jax.ShapeDtypeStruct((8, TILES), jnp.int32),
            jax.ShapeDtypeStruct((ROWS // 2, LANES), F32),
            jax.ShapeDtypeStruct((ROWS // 2, LANES), F32),
        )
        + (jax.ShapeDtypeStruct((ROWS, LANES), F32),) * 5,
        scratch_shapes=[pltpu.VMEM(x.shape, x.dtype) for x in inputs[5:]]
        + [
            pltpu.VMEM(((SLOTS + 8) * 16, LANES), F32),
            pltpu.SMEM((8, TILES), jnp.int32),
            pltpu.SemaphoreType.DMA(()),
            pltpu.SemaphoreType.DMA((11,)),
        ],
        compiler_params=pltpu.CompilerParams(vmem_limit_bytes=VMEM_BYTES),
        name="pack",
    )(*(pltpu.with_memory_space_constraint(x, pltpu.HBM) for x in inputs))


def unpack_tile_kernel(pos_ref, recv_ref, temp_ref, sea_west_ref, sea_east_ref, tile_ref, west_ref, east_ref):
    chunk = lane_ids() // HALO

    def band(i):
        base = i * 64
        rows = slice(8 * i, 8 * i + 8)
        quads = []
        for h in range(2):
            four = []
            for k in range(4 * i, 4 * i + 4):
                got = recv_ref[pos_ref[0, k], h * FIELDS : (h + 1) * FIELDS, :]
                four.append(jnp.where(pos_ref[1, k] > 0, got, 0.0))
            quads.append(four)
        quads = yield from swap_chunks(quads)
        for h in range(2):
            for r, x in enumerate(quads[h]):
                tile_ref[pl.ds(base + h * 4 + r, FIELDS, stride=8), :] = x
        melt = jnp.exp(-0.5 * jnp.maximum(temp_ref[rows, :], 0.0))
        yield
        moved = []
        for f in range(FIELDS):
            at = slice(base + 8 * f, base + 8 * f + 8)
            x = tile_ref[at, :]
            if f == 5:
                x = x * melt
                tile_ref[at, :] = x
            moved.append(roll(x, f * HALO))
        yield
        west, east = moved[0], moved[0]
        for f in range(1, FIELDS):
            west = jnp.where(chunk == f, moved[f], west)
            east = jnp.where(chunk == f - 1, moved[f], east)
        west_ref[rows, :] = west
        east_ref[rows, :] = east

    interleave([band(i) for i in range(BANDS)], 5)
    west_ref[ROWS:, :] = sea_west_ref[...]
    east_ref[ROWS:, :] = sea_east_ref[...]


EDGE = ROWS + ROWS // 2


def unpack_tile(pos, recv, temp, sea_west, sea_east):
    return pl.pallas_call(
        unpack_tile_kernel,
        in_specs=specs(5),
        out_shape=(
            jax.ShapeDtypeStruct((BANDS * FIELDS * 8, LANES), F32),
            jax.ShapeDtypeStruct((EDGE, LANES), F32),
            jax.ShapeDtypeStruct((EDGE, LANES), F32),
        ),
        compiler_params=pltpu.CompilerParams(vmem_limit_bytes=VMEM_BYTES),
        name="unpack_tile",
    )(pos, recv, temp, sea_west, sea_east)


STATE = ("u", "v", "p", "m", "t")
STATIC = ("ou", "ov", "wx", "wy", "inertia", "turn", "k", "cover")


def put_ice(s, i, ice, row_ids, grid_rows):
    u, v, total, diff, shear, strength, mass, cover = ice
    at = slice(8 + 8 * i, 16 + 8 * i)
    here = slice(8 * i, 8 * i + 8)
    s["u"][at, :] = u
    s["v"][at, :] = v
    s["p"][at, :] = cover * (total + diff)
    s["m"][at, :] = cover * (total - diff)
    s["t"][at, :] = cover * (shear + shear)
    coriolis = 2.0 * (row_ids.astype(F32) + 0.5) / grid_rows - 1.0
    s["inertia"][here, :] = 2.0 * mass
    s["turn"][here, :] = mass * coriolis
    s["k"][here, :] = (0.4 * I14) * (cover * strength)
    s["cover"][here, :] = cover


def put_ocean(s, i, ocean):
    here = slice(8 * i, 8 * i + 8)
    for name, x in zip(("ou", "ov", "wx", "wy"), ocean):
        s[name][here, :] = x


def clear_ends(s, chunks):
    zero = jnp.zeros((8, LANES), F32)
    for name in STATE:
        s[name][0:8, :] = zero
        s[name][8 + 8 * chunks : 16 + 8 * chunks, :] = zero


def run_subcycles(s, chunks, times):
    def subcycle(step, carry):
        for i in chunks:
            a = 8 + 8 * i
            at, up, down = slice(a, a + 8), slice(a + 1, a + 9), slice(a - 1, a + 7)
            here = slice(8 * i, 8 * i + 8)
            u, v = s["u"][at, :], s["v"][at, :]
            exx = roll(u, -1) - roll(u, 1)
            eyy = s["v"][up, :] - s["v"][down, :]
            shear = (s["u"][up, :] - s["u"][down, :]) + (roll(v, -1) - roll(v, 1))
            div = exx + eyy
            ten = exx - eyy
            q = div * div + 0.25 * (ten * ten + shear * shear) + 0.04
            inv = lax.rsqrt(q)
            k = s["k"][here, :] * inv
            base = div - q * inv
            ten = 0.25 * ten
            s["p"][at, :] = I14 * s["p"][at, :] + k * (base + ten)
            s["m"][at, :] = I14 * s["m"][at, :] + k * (base - ten)
            s["t"][at, :] = I14 * s["t"][at, :] + (0.25 * k) * shear
        for i in chunks:
            a = 8 + 8 * i
            at, up, down = slice(a, a + 8), slice(a + 1, a + 9), slice(a - 1, a + 7)
            here = slice(8 * i, 8 * i + 8)
            p, t = s["p"][at, :], s["t"][at, :]
            fx = 0.25 * ((roll(p, -1) - roll(p, 1)) + (s["t"][up, :] - s["t"][down, :]))
            fy = 0.25 * ((roll(t, -1) - roll(t, 1)) + (s["m"][up, :] - s["m"][down, :]))
            u, v = s["u"][at, :], s["v"][at, :]
            ou, ov = s["ou"][here, :], s["ov"][here, :]
            du, dv = ou - u, ov - v
            g = du * du + dv * dv + 0.01
            drag = g * lax.rsqrt(g)
            inertia, turn = s["inertia"][here, :], s["turn"][here, :]
            diag = inertia + drag
            rx = inertia * u + fx + s["wx"][here, :] + drag * ou
            ry = inertia * v + fy + s["wy"][here, :] + drag * ov
            w = s["cover"][here, :] / (diag * diag + turn * turn)
            s["u"][at, :] = w * (diag * rx + turn * ry)
            s["v"][at, :] = w * (diag * ry - turn * rx)
        return carry

    lax.fori_loop(0, times, subcycle, 0)


def state_scratch(chunks):
    tall = pltpu.VMEM((8 * chunks + 16, LANES), F32)
    flat = pltpu.VMEM((8 * chunks, LANES), F32)
    return [tall] * len(STATE) + [flat] * len(STATIC)


def named(scratch):
    return dict(zip(STATE + STATIC, scratch))


def at_row(i):
    return lax.axis_index("gy") * ROWS + 8 * i + lax.broadcasted_iota(jnp.int32, (8, LANES), 0)


def chunk_of(tile_ref, i):
    return [tile_ref[i * 64 + f * 8 : i * 64 + f * 8 + 8, :] for f in range(FIELDS)]


def stresses(p, m, t):
    return 0.5 * (p + m), 0.5 * (p - m), 0.5 * t


def finals(s, i):
    at = slice(8 + 8 * i, 16 + 8 * i)
    return [s["u"][at, :], s["v"][at, :], *stresses(s["p"][at, :], s["m"][at, :], s["t"][at, :])]


def inner_kernel(tile_ref, ou_ref, ov_ref, wx_ref, wy_ref, out_ref, *scratch):
    s = named(scratch)
    grid_rows = ROWS * lax.axis_size("gy")
    clear_ends(s, BANDS)
    for i in range(BANDS):
        put_ice(s, i, chunk_of(tile_ref, i), at_row(i), grid_rows)
        put_ocean(s, i, [ref[8 * i : 8 * i + 8, :] for ref in (ou_ref, ov_ref, wx_ref, wy_ref)])
    run_subcycles(s, range(BANDS), SUBS)
    for i in range(BANDS):
        for f, x in enumerate(finals(s, i)):
            out_ref[f, 8 * i : 8 * i + 8, :] = x


def inner(tile, ocean):
    return pl.pallas_call(
        inner_kernel,
        out_shape=jax.ShapeDtypeStruct((FINAL, ROWS, LANES), F32),
        scratch_shapes=state_scratch(BANDS),
        compiler_params=pltpu.CompilerParams(vmem_limit_bytes=VMEM_BYTES),
        cost_estimate=pl.CostEstimate(flops=4_000_000, bytes_accessed=4_000_000, transcendentals=800_000),
        name="inner",
    )(tile, *ocean)


def strip_moves(own, west, east, chunk):
    return own, roll(own, -32), roll(west, (8 - chunk) * HALO), roll(east, (6 - chunk) * HALO)


def strip(own, moved, west, east, lane):
    x = jnp.where(lane < 48, own, moved)
    x = jnp.where(lane >= 112, west, x)
    return jnp.where((lane >= 96) & (lane < 112), east, x)


def ice_strips(own, west, east, edge, lane):
    west = jnp.where(edge[0], 0.0, west)
    east = jnp.where(edge[1], 0.0, east)
    moved = [strip_moves(own[f], west, east, f) for f in range(FIELDS)]
    yield
    return [strip(*x, lane) for x in moved]


def ocean_strips(own, west, east, half, lane):
    moved = [strip_moves(own[f], west, east, 4 * half + f) for f in range(4)]
    yield
    return [strip(*x, lane) for x in moved]


def edges_x():
    a = lax.axis_index("gx")
    return a == 0, a == lax.axis_size("gx") - 1


def edges_y():
    b = lax.axis_index("gy")
    return b == 0, b == lax.axis_size("gy") - 1


def join(mid, strips, moved, lane):
    x = jnp.where(lane < HALO, strips, mid)
    return jnp.where(lane >= LANES - HALO, moved, x)


def finish_band(band, mids, strips, refs, stage, lane):
    pos_ref, tile_ref, ou_ref, ov_ref, packed_ref, drag_ref = refs
    moved = [roll(x, 32) for x in strips]
    yield
    five = [join(*x, lane) for x in zip(mids, strips, moved)]
    for f, x in enumerate(five):
        for h in range(2):
            at = h * FINAL * 4 + f * 4
            stage[at : at + 4, :] = x[4 * h : 4 * h + 4, :]
    rows = slice(8 * band, 8 * band + 8)
    cover = tile_ref[band * 64 + 56 : band * 64 + 64, :]
    drag_ref[0, rows, :], drag_ref[1, rows, :] = drag_rows(five, ou_ref[rows, :], ov_ref[rows, :], cover)
    yield
    quad = [stage[pl.ds(r, 2 * FINAL, stride=4), :] for r in range(4)]
    (quad,) = yield from swap_chunks([quad])
    for c, x in enumerate(quad):
        packed_ref[pl.ds(pos_ref[0, band * 4 + c] * 2 * FINAL, 2 * FINAL), :] = x


def drag_rows(five, ou, ov, cover):
    du, dv = five[0] - ou, five[1] - ov
    g = du * du + dv * dv + 0.01
    drag = cover * (g * lax.rsqrt(g))
    return drag * du, drag * dv


def sides_kernel(
    pos_ref, tile_ref, west_ref, east_ref, ou_ref, ov_ref, wx_ref, wy_ref, mid_ref, packed_ref, drag_ref, stage, *scratch,
):
    s = named(scratch)
    lane = lane_ids()
    grid_rows = ROWS * lax.axis_size("gy")
    edge = edges_x()
    clear_ends(s, BANDS)

    def start(i):
        rows = slice(8 * i, 8 * i + 8)
        ice = yield from ice_strips(chunk_of(tile_ref, i), west_ref[rows, :], east_ref[rows, :], edge, lane)
        put_ice(s, i, ice, at_row(i), grid_rows)
        half, j = divmod(i, BANDS // 2)
        sea = slice(ROWS + 8 * j, ROWS + 8 * j + 8)
        own = [ref[rows, :] for ref in (ou_ref, ov_ref, wx_ref, wy_ref)]
        put_ocean(s, i, (yield from ocean_strips(own, west_ref[sea, :], east_ref[sea, :], half, lane)))

    interleave([start(i) for i in range(BANDS)], 3)
    run_subcycles(s, range(BANDS), SUBS)
    refs = (pos_ref, tile_ref, ou_ref, ov_ref, packed_ref, drag_ref)

    def finish(i):
        mids = [mid_ref[f, 8 * i : 8 * i + 8, :] for f in range(FINAL)]
        yield from finish_band(i, mids, finals(s, i), refs, stage.at[i], lane)

    interleave([finish(i) for i in range(2, BANDS - 2)], 6)


def stage_scratch(bands):
    return [pltpu.VMEM((bands, 2 * FINAL * 4, LANES), F32)]


RESULTS = (
    jax.ShapeDtypeStruct((2 * TILES * 2 * FINAL, LANES), F32),
    jax.ShapeDtypeStruct((2, ROWS, LANES), F32),
)


def sides(pos, tile, west, east, ocean, mid):
    return pl.pallas_call(
        sides_kernel,
        in_specs=specs(9),
        out_shape=RESULTS,
        scratch_shapes=stage_scratch(BANDS) + state_scratch(BANDS),
        compiler_params=pltpu.CompilerParams(vmem_limit_bytes=VMEM_BYTES),
        cost_estimate=pl.CostEstimate(flops=5_000_000, bytes_accessed=5_000_000, transcendentals=800_000),
        name="sides",
    )(pos, tile, west, east, *ocean, mid)


def ends_kernel(
    pos_ref, tile_ref, west_ref, east_ref, north_ref, south_ref, ou_ref, ov_ref, wx_ref, wy_ref,
    packed_in, drag_in, packed_ref, drag_ref, stage, *scratch,
):
    packed_ref[...] = packed_in[...]
    drag_ref[...] = drag_in[...]
    s = named(scratch)
    lane = lane_ids()
    grid_rows = ROWS * lax.axis_size("gy")
    edge = edges_x()
    outside = edges_y()
    ocean_refs = (ou_ref, ov_ref, wx_ref, wy_ref)
    clear_ends(s, 24)

    def start(end, j):
        ref = (north_ref, south_ref)[end]
        i = (j - 2) if end == 0 else BANDS - 4 + j
        half = 1 - end if not 0 <= i < BANDS else i // (BANDS // 2)
        if 0 <= i < BANDS:
            rows = slice(8 * i, 8 * i + 8)
            own = chunk_of(tile_ref, i)
            west, east = west_ref[rows, :], east_ref[rows, :]
            water = [x[rows, :] for x in ocean_refs]
            at = ROWS + 8 * (i % (BANDS // 2))
            sea_west, sea_east = west_ref[at : at + 8, :], east_ref[at : at + 8, :]
        else:
            at = 8 * (i % 2)

            def part_of(base):
                return ref[base + at : base + at + 8, :]

            own = [jnp.where(outside[end], 0.0, x) for x in chunk_of(ref, i % 2)]
            west = jnp.where(outside[end], 0.0, part_of(128))
            east = jnp.where(outside[end], 0.0, part_of(144))
            water = [part_of(160 + 16 * f) for f in range(4)]
            sea_west, sea_east = part_of(224), part_of(240)
        for part in range(2):
            chunk = part * 12 + end * 6 + j
            ice = (yield from ice_strips(own, west, east, edge, lane)) if part else own
            put_ice(s, chunk, ice, at_row(i), grid_rows)
            if part:
                water = yield from ocean_strips(water, sea_west, sea_east, half, lane)
            put_ocean(s, chunk, water)

    interleave([start(end, j) for end in range(2) for j in range(6)], 3)
    run_subcycles(s, range(24), SUBS // 2)
    run_subcycles(s, [c for c in range(24) if c % 6 not in (0, 5)], SUBS // 2)
    refs = (pos_ref, tile_ref, ou_ref, ov_ref, packed_ref, drag_ref)

    def finish(n):
        end, j = divmod(n, 2)
        chunk = end * 6 + j + 2
        i = BANDS - 2 + j if end else j
        yield from finish_band(i, finals(s, chunk), finals(s, chunk + 12), refs, stage.at[n], lane)

    interleave([finish(n) for n in range(4)], 4)


def ends(pos, tile, west, east, north, south, ocean, packed, drag):
    return pl.pallas_call(
        ends_kernel,
        in_specs=specs(12),
        out_shape=RESULTS,
        scratch_shapes=stage_scratch(4) + state_scratch(24),
        compiler_params=pltpu.CompilerParams(vmem_limit_bytes=VMEM_BYTES),
        name="ends",
    )(pos, tile, west, east, north, south, *ocean, packed, drag)


def unpack_ice_kernel(starts_ref, recv_ref, vel_ref, str_ref, blk):
    for t in range(TILES):
        start = starts_ref[0, t]
        for c in range(2):
            at = (2 * t + c) * 2 * FINAL
            to = pl.multiple_of((start + c) * 16, 16)
            blk[pl.ds(to, 2 * FINAL), :] = recv_ref[at : at + 2 * FINAL, :]
    for g in range(SLOTS // 8):
        eight = slice(8 * g, 8 * g + 8)
        for h in range(2):
            cut = slice(h * LANES, (h + 1) * LANES)
            for f in range(3):
                str_ref[f, eight, cut] = blk[pl.ds(128 * g + h * FINAL + 2 + f, 8, stride=16), :]
            for j in range(8):
                at = 128 * g + 16 * j + h * FINAL
                vel_ref[8 * g + j, :, cut] = blk[at : at + 2, :]


def unpack_ice(starts, recv):
    vel, strs = pl.pallas_call(
        unpack_ice_kernel,
        in_specs=specs(2),
        out_shape=(
            jax.ShapeDtypeStruct((SLOTS, 2, 2 * LANES), F32),
            jax.ShapeDtypeStruct((3, SLOTS, 2 * LANES), F32),
        ),
        scratch_shapes=[pltpu.VMEM(((SLOTS + 8) * 16, LANES), F32)],
        compiler_params=pltpu.CompilerParams(vmem_limit_bytes=VMEM_BYTES),
        name="unpack_ice",
    )(starts, recv)
    return vel, jnp.transpose(strs, (1, 0, 2))


def both_ways(axis, forward, backward):
    n = lax.axis_size(axis)
    return (
        lax.ppermute(forward, axis, [(i, (i + 1) % n) for i in range(n)]),
        lax.ppermute(backward, axis, [((i + 1) % n, i) for i in range(n)]),
    )


def on_device(
    owner_list, ice_mask, velocity, stress, thickness, concentration, ocean_u, ocean_v, wind_x, wind_y, surface_temp
):
    ocean = (ocean_u, ocean_v, wind_x, wind_y)
    outbound, starts, pos, sea_west, sea_east, *maps = pack(
        owner_list, ice_mask, velocity, stress, thickness, concentration, (*ocean, surface_temp)
    )
    *ocean, surface_temp = maps
    arrived = lax.all_to_all(outbound, AXES, split_axis=0, concat_axis=0, tiled=True)
    tile, west_edge, east_edge = unpack_tile(pos, arrived, surface_temp, sea_west, sea_east)
    west, east = both_ways("gx", east_edge, west_edge)
    west, east, mid = lax.optimization_barrier((west, east, inner(tile, ocean)))

    def edge(cells, block_rows, sea_rows):
        parts = [tile[block_rows], west[:ROWS][cells], east[:ROWS][cells]]
        parts += [x[cells] for x in ocean] + [west[sea_rows], east[sea_rows]]
        return jnp.concatenate(parts, axis=0)

    low = edge(slice(0, HALO), slice(0, 128), slice(ROWS, ROWS + HALO))
    high = edge(slice(ROWS - HALO, ROWS), slice(-128, None), slice(EDGE - HALO, EDGE))
    north, south = both_ways("gy", high, low)
    packed, drag = sides(pos, tile, west, east, ocean, mid)
    packed, drag = ends(pos, tile, west, east, north, south, ocean, packed, drag)

    homeward = packed.reshape(2 * TILES, FINAL, 2, LANES)
    back = lax.all_to_all(homeward, AXES, split_axis=0, concat_axis=0, tiled=True)
    vel, strs = unpack_ice(starts, back.reshape(2 * TILES * 2 * FINAL, LANES))
    return vel, strs, drag


def solution(mesh):
    blocks = P(AXES, None, None)
    return jax.shard_map(
        on_device,
        mesh=mesh,
        in_specs=(P(), P(AXES, None)) + (blocks,) * 4 + (P("gy", "gx"),) * 5,
        out_specs=(blocks, blocks, P(None, "gy", "gx")),
        check_vma=False,
    )
```

time: 124 us -> 101 us (0.81)
  blocking collectives: 31 us -> 72.1 us
  waiting for transfers between devices: 25.5 us -> 0.72 us
  starting transfers between devices: 27.3 us -> 6.7 us
  Pallas kernels: 33.9 us -> 20.6 us
  local copies, waits for them, and re-layouts: 5.32 us -> 0.04 us
    all_to_all x0 -> x1, blocking collectives: none -> 41.8 us  [on_device(): lax.all_to_all(outbound, AXES, split_axis=0, concat_axis=0, tiled=True)]
    ppermute x4 -> x2, waiting for transfers between devices: 25.5 us -> 0.71 us  [both_ways(): lax.ppermute(forward, axis, [(i, (i + 1) % n) for i in range(n)])]
    pallas_call x5 -> x4, Pallas kernels: 29 us -> 15.6 us  [the longest x1 6.43 us: sides(): pl.pallas_call(sides_kernel, in_specs=specs(9), out_shape=RESULTS, scratc...]
    all_to_all x1 -> x0, starting transfers between devices: 11.5 us -> none  [on_device(): lax.all_to_all(outbound, AXES, split_axis=0, concat_axis=0, tiled=True)]
    ppermute x4 -> x2, starting transfers between devices: 6.85 us -> 0.08 us  [both_ways(): lax.ppermute(forward, axis, [(i, (i + 1) % n) for i in range(n)])]
    unnamed x28 -> x8, local copies, waits for them, and re-layouts: 5.31 us -> 0.04 us
    ppermute x4 -> x2, starting transfers between devices: 8.96 us -> 6.63 us  [both_ways(): lax.ppermute(backward, axis, [((i + 1) % n, i) for i in range(n)])]
  transfers between devices with their start and end apart: 9 -> 4, of which waited for: 2 -> 1; matrix products, arithmetic and copies ran while one was open for 0% -> 0% of each run, Pallas kernels for 14% -> 10%
where the time goes in v1:
time: 101 us
  blocking collectives  72.1 us (71%)
  Pallas kernels  20.6 us (20%)
  starting transfers between devices  6.7 us (7%)
    all_to_all x1, blocking collectives, on_device(): lax.all_to_all(outbound, AXES, split_axis=0, concat_axis=0, tiled=True)  41.8 us
    all_to_all x1, blocking collectives, on_device(): lax.all_to_all(homeward, AXES, split_axis=0, concat_axis=0, tiled=True)  30.3 us
    ppermute x2, starting transfers between devices, both_ways(): lax.ppermute(backward, axis, [((i + 1) % n, i) for i in range(n)])  6.63 us
    pallas_call x1, Pallas kernels, sides(): pl.pallas_call(sides_kernel, in_specs=specs(9), out_shape=RESULTS, scratc...  6.43 us
    pallas_call x1, Pallas kernels, ends(): pl.pallas_call(ends_kernel, in_specs=specs(12), out_shape=RESULTS, scratc...  4.25 us
    pallas_call x1, Pallas kernels, inner(): pl.pallas_call(inner_kernel, out_shape=jax.ShapeDtypeStruct((FINAL, ROWS,...  3.27 us
    pallas_call x1, Pallas kernels, unpack_tile(): pl.pallas_call(unpack_tile_kernel, in_specs=specs(5), out_shape=(jax.Shap...  2.68 us
    pallas_call x1, Pallas kernels, pack(): pl.pallas_call(pack_kernel, in_specs=[pl.BlockSpec(memory_space=pltpu.HBM...  2.22 us
  transfers between devices with their start and end apart: 4, of which 1 were waited for; matrix products, arithmetic and copies ran while one was open for 0% of the time, Pallas kernels for 10%

profile of v1, /device:TPU:1, one launch (start us, length us, event | category | flops | bytes accessed | tf_op | source)
XLA Modules:
  0.0 100.9 jit_solution(17001904747228773816)
XLA Ops:
  0.6 2.2 %pack.1 = (f32[256,16,128]{2,1,0:T(8,128)S(1)}, s32[8,128]{1,0:T(8,128)S(1)}, s32[8,128]{1,0:T(8,128)S(1)}, f32[128,128]{1,0:T(8,128)S(1)}, f32[128,128]{1,0:T(8...) custom-call(f32[256,128]{1,0:T(8,128)} %refs_0_.1, ...), custom_call_target="tpu_custom_call" | custom-call | tf_op jit(solution)/shard_map/pack/pallas_call | solution.py:152
  2.9 41.8 %all_to_all.10.recv_ref = f32[256,16,128]{2,1,0:T(8,128)S(1)} all-to-all(f32[256,16,128]{2,1,0:T(8,128)S(1)} %get-tuple-element.27), channel_id=1, replica_groups=mesh['gx'=16,'gy'=8] {'gx','gy'}, dimensions={0} | all-to-all | bytes 4194304 | tf_op jit(solution)/shard_map/all_to_all | solution.py:594
  44.7 2.7 %unpack_tile.1 = (f32[2048,128]{1,0:T(8,128)S(1)}, f32[384,128]{1,0:T(8,128)S(1)}, f32[384,128]{1,0:T(8,128)S(1)}) custom-call(s32[8,128]{1,0:T(8,128)S(1)} %get-tuple-element.26.pos_ref, f32[256,16,128]{2,1,0:T(8,128)S(1)} %all_to_all.10.recv_ref, f32[256,128]{1,0:T(8,128)S(1)} %get-tuple-element.28.temp_ref, ...), custom_call_target="tpu_custom_call" | custom-call | tf_op jit(solution)/shard_map/unpack_tile/pallas_call | solution.py:219
  47.4 0.1 collective-permute-start
  47.5 4.8 %collective-permute-start.1 = (f32[384,128]{1,0:T(8,128)S(1)}, f32[384,128]{1,0:T(8,128)S(1)}, u32[]{:S(2)}, u32[]{:S(2)}) collective-permute-start(f32[384,128]{1,0:T(8,128)S(1)} %get-tuple-element.33), channel_id=1, source_target_pairs={{8,0},{16,8},{24,16},{32,24},{40,32},{48,40},{56,48},{64,56},{72,6... | collective-permute-start | bytes 589832 | tf_op jit(solution)/shard_map/ppermute | solution.py:582
  52.2 3.3 %inner.1.mid_ref = f32[5,256,128]{2,1,0:T(8,128)S(1)} custom-call(f32[2048,128]{1,0:T(8,128)S(1)} %get-tuple-element.31.tile_ref, f32[256,128]{1,0:T(8,128)S(1)} %get-tuple-element.34.ou_ref, f32[256,128]{1,0:T(8,128)S(1)} %get-tuple-element.35.ov_ref, f32[256,128]{1,0:T(8,128)S(1)} %get-tuple-element.36.wx_ref, f32[256,128]{1,0:T(8,128)S(1)} %get-tuple-element.37.wy_ref), custom_call_target="tpu_custom_call" | custom-call | flops 4000000 | bytes 4000000 | tf_op jit(solution)/shard_map/inner/pallas_call | solution.py:350
  55.5 0.7 collective-permute-done.west_ref
  56.2 0.0 collective-permute-done.1.east_ref
  56.3 1.9 %collective-permute-start.3 = (f32[256,128]{1,0:T(8,128)S(1)}, f32[256,128]{1,0:T(8,128)S(1)}, u32[]{:S(2)}, u32[]{:S(2)}) collective-permute-start(f32[256,128]{1,0:T(8,128)S(1)} %get-tuple-element.49), channel_id=1, source_target_pairs={{1,0},{2,1},{3,2},{4,3},{5,4},{6,5},{7,6},{0,7},{9,8},{10,9},{11,1... | collective-permute-start | bytes 393224 | tf_op jit(solution)/shard_map/ppermute | solution.py:582
  58.2 0.0 collective-permute-start.2
  58.2 6.4 %sides.1 = (f32[2560,128]{1,0:T(8,128)S(1)}, f32[2,256,128]{2,1,0:T(8,128)S(1)}) custom-call(s32[8,128]{1,0:T(8,128)S(1)} %get-tuple-element.26.pos_ref, f32[2048,128]{1,0:T(8,128)S(1)} %get-tuple-element.31.tile_ref, f32[384,128]{1,0:T(8,128)S(1)} %collective-permute-done.west_ref, f32[384,128]{1,0:T(8,128)S(1)} %collective-permute-done.1.east_ref, ...), custom_call_target="tpu_custom_call" | custom-call | flops 5000000 | bytes 5000000 | tf_op jit(solution)/shard_map/sides/pallas_call | solution.py:465
  64.6 0.0 collective-permute-done.3.south_ref
  64.6 0.0 collective-permute-done.2.north_ref
  64.6 4.3 %ends.1 = (f32[2560,128]{1,0:T(8,128)S(1)}, f32[2,256,128]{2,1,0:T(8,128)}) custom-call(s32[8,128]{1,0:T(8,128)S(1)} %get-tuple-element.26.pos_ref, f32[2048,128]{1,0:T(8,128)S(1)} %get-tuple-element.31.tile_ref, f32[384,128]{1,0:T(8,128)S(1)} %collective-permute-done.west_ref, f32[384,128]{1,0:T(8,128)S(1)} %collective-permute-done.1.east_ref, ...), custom_call_target="tpu_custom_call" | custom-call | tf_op jit(solution)/shard_map/ends/pallas_call | solution.py:535
  68.9 30.3 %all_to_all.11 = f32[256,5,2,128]{3,2,1,0:T(2,128)S(1)} all-to-all(f32[256,5,2,128]{3,2,1,0:T(2,128)S(1)} %bitcast.7), channel_id=1, replica_groups=mesh['gx'=16,'gy'=8] {'gx','gy'}, dimensions={0} | all-to-all | bytes 2621440 | tf_op jit(solution)/shard_map/all_to_all | solution.py:611
  99.2 1.7 %unpack_ice.1 = (f32[112,2,256]{2,1,0:T(2,128)}, f32[3,112,256]{2,1,0:T(8,128)}) custom-call(s32[8,128]{1,0:T(8,128)S(1)} %get-tuple-element.25.starts_ref, f32[2560,128]{1,0:T(8,128)S(1)} %bitcast.6), custom_call_target="tpu_custom_call" | custom-call | tf_op jit(solution)/shard_map/unpack_ice/pallas_call | solution.py:564
  (9 shorter events, 0.0 us)
Async XLA Ops:
  47.4 8.9 %collective-permute-start = (f32[384,128]{1,0:T(8,128)S(1)}, f32[384,128]{1,0:T(8,128)S(1)}, u32[]{:S(2)}, u32[]{:S(2)}) collective-permute-start(f32[384,128]{1,0:T(8,128)S(1)} %get-tuple-element.32), channel_id=1, source_target_pairs={{0,8},{8,16},{16,24},{24,32},{32,40},{40,48},{48,56},{56,64},{64,7... | collective-permute-start | bytes 589832 | tf_op jit(solution)/shard_map/ppermute | solution.py:581
  47.5 8.8 %collective-permute-start.1 = (f32[384,128]{1,0:T(8,128)S(1)}, f32[384,128]{1,0:T(8,128)S(1)}, u32[]{:S(2)}, u32[]{:S(2)}) collective-permute-start(f32[384,128]{1,0:T(8,128)S(1)} %get-tuple-element.33), channel_id=1, source_target_pairs={{8,0},{16,8},{24,16},{32,24},{40,32},{48,40},{56,48},{64,56},{72,6... | collective-permute-start | bytes 589832 | tf_op jit(solution)/shard_map/ppermute | solution.py:582
  56.3 8.3 %collective-permute-start.3 = (f32[256,128]{1,0:T(8,128)S(1)}, f32[256,128]{1,0:T(8,128)S(1)}, u32[]{:S(2)}, u32[]{:S(2)}) collective-permute-start(f32[256,128]{1,0:T(8,128)S(1)} %get-tuple-element.49), channel_id=1, source_target_pairs={{1,0},{2,1},{3,2},{4,3},{5,4},{6,5},{7,6},{0,7},{9,8},{10,9},{11,1... | collective-permute-start | bytes 393224 | tf_op jit(solution)/shard_map/ppermute | solution.py:582
  58.2 6.5 %collective-permute-start.2 = (f32[256,128]{1,0:T(8,128)S(1)}, f32[256,128]{1,0:T(8,128)S(1)}, u32[]{:S(2)}, u32[]{:S(2)}) collective-permute-start(f32[256,128]{1,0:T(8,128)S(1)} %get-tuple-element.50), channel_id=1, source_target_pairs={{0,1},{1,2},{2,3},{3,4},{4,5},{5,6},{6,7},{7,0},{8,9},{9,10},{10,1... | collective-permute-start | bytes 393224 | tf_op jit(solution)/shard_map/ppermute | solution.py:581

commit v2 on v1

--- a/solution.py
+++ b/solution.py
@@ -29,7 +29,7 @@
 
 
 def roll(x, shift):
-    return pltpu.roll(x, shift % LANES, 1)
+    return pltpu.roll(x, shift % LANES, 1) if shift % LANES else x
 
 
 def interleave(tasks, width):
@@ -48,30 +48,35 @@
         active = running
 
 
-def swap_chunks(quads):
-    lane = lane_ids(quads[0][0].shape[0])
-    low, even = lane < 64, (lane & 32) == 0
-    far = [(roll(jnp.where(low, c, a), 64), roll(jnp.where(low, d, b), 64)) for a, b, c, d in quads]
+def swap_chunks(quads, room):
+    chunk = lane_ids() // 32
+    moved = [[roll(x, 32 * c) for c, x in enumerate(quad)] for quad in quads]
     yield
-    quads = [
-        (jnp.where(low, a, ac), jnp.where(low, b, bd), jnp.where(low, ac, c), jnp.where(low, bd, d))
-        for (a, b, c, d), (ac, bd) in zip(quads, far)
-    ]
-    near = [(roll(b, 32), roll(a, 96), roll(d, 32), roll(c, 96)) for a, b, c, d in quads]
+    for q, quad in enumerate(moved):
+        for c, x in enumerate(quad):
+            room[q, c] = x
     yield
-    return [
-        (jnp.where(even, a, p), jnp.where(even, q, b), jnp.where(even, c, r), jnp.where(even, t, d))
-        for (a, b, c, d), (p, q, r, t) in zip(quads, near)
-    ]
+    out = []
+    for q in range(len(quads)):
+        kept = [room[q, c] for c in range(4)]
+        rows = []
+        for r in range(4):
+            x = kept[-r % 4]
+            for to in range(1, 4):
+                x = jnp.where(chunk == to, kept[(to - r) % 4], x)
+            rows.append(roll(x, -32 * r))
+        out.append(rows)
+    yield
+    return out
 
 
 def pack_kernel(*refs):
     far, refs = refs[:11], refs[11:]
     (out_ref, starts_ref, pos_ref, west_ref, east_ref), refs = refs[:5], refs[5:]
-    here, (blk, near, sem, sems) = refs[:11], refs[11:]
+    here, (blk, starts_v, pos_v, scalars, sems) = refs[:11], refs[11:]
     ou_ref, ov_ref, wx_ref, wy_ref, _, owner_ref, con_ref, thk_ref, str_ref, mask_ref, vel_ref = here
     loads = [pltpu.make_async_copy(x, y, sems.at[n]) for n, (x, y) in enumerate(zip(far, here))]
-    for n in (*range(5, 11), *range(5)):
+    for n in (5, 0, 1, 2, 3, 6, 7, 8, 9, 10, 4):
         loads[n].start()
     loads[5].wait()
     me = lax.axis_index("gx") * lax.axis_size("gy") + lax.axis_index("gy")
@@ -82,9 +87,9 @@
     owned = jnp.where(owner_ref[...] == me, 1.0, 0.0)
     counts = lax.dot_general(ones, owned, (((1,), (1,)), ((), ())), preferred_element_type=F32)
     starts = jnp.dot(counts, before, preferred_element_type=F32)
-    starts_ref[...] = starts.astype(jnp.int32)
-    copy = pltpu.make_async_copy(starts_ref, near, sem)
-    copy.start()
+    starts_v[...] = starts.astype(jnp.int32)
+    starts_copy = pltpu.make_async_copy(starts_v, starts_ref, scalars.at[0])
+    starts_copy.start()
 
     mine = jnp.broadcast_to(owner_ref[pl.ds(me, 1), :], (TILES, TILES)).astype(F32)
     column = mine.T
@@ -96,7 +101,29 @@
     icy = mine < TILES
     slot = jnp.where(icy, 2.0 * mine + rank, 2.0 * free + 1.0)
     row = lax.broadcasted_iota(jnp.int32, (8, TILES), 0)
-    pos_ref[...] = jnp.where(row == 0, slot, jnp.where(icy, 1.0, 0.0)).astype(jnp.int32)
+    pos_v[...] = jnp.where(row == 0, slot, jnp.where(icy, 1.0, 0.0)).astype(jnp.int32)
+    pos_copy = pltpu.make_async_copy(pos_v, pos_ref, scalars.at[1])
+    pos_copy.start()
+
+    for n in range(4):
+        loads[n].wait()
+    chunk = lane_ids() // HALO
+
+    def sea_edges(i):
+        moved = []
+        for half in range(2):
+            rows = slice(8 * i + half * LANES, 8 * i + half * LANES + 8)
+            for f, ref in enumerate((ou_ref, ov_ref, wx_ref, wy_ref)):
+                moved.append(roll(ref[rows, :], (4 * half + f) * HALO))
+        yield
+        west, east = moved[0], moved[0]
+        for n in range(1, 8):
+            west = jnp.where(chunk == n, moved[n], west)
+            east = jnp.where(chunk == n - 1, moved[n], east)
+        west_ref[8 * i : 8 * i + 8, :] = west
+        east_ref[8 * i : 8 * i + 8, :] = east
+
+    interleave([sea_edges(i) for i in range(BANDS // 2)], 5)
 
     for n in range(6, 11):
         loads[n].wait()
@@ -115,29 +142,11 @@
                 at = 128 * g + 16 * j + 8 * h
                 blk[at : at + 2, :] = vel_ref[8 * g + j, :, cut]
 
-    for n in range(5):
-        loads[n].wait()
-    chunk = lane_ids() // HALO
-
-    def sea_edges(i):
-        moved = []
-        for half in range(2):
-            rows = slice(8 * i + half * LANES, 8 * i + half * LANES + 8)
-            for f, ref in enumerate((ou_ref, ov_ref, wx_ref, wy_ref)):
-                moved.append(roll(ref[rows, :], (4 * half + f) * HALO))
-        yield
-        west, east = moved[0], moved[0]
-        for n in range(1, 8):
-            west = jnp.where(chunk == n, moved[n], west)
-            east = jnp.where(chunk == n - 1, moved[n], east)
-        west_ref[8 * i : 8 * i + 8, :] = west
-        east_ref[8 * i : 8 * i + 8, :] = east
-
-    interleave([sea_edges(i) for i in range(BANDS // 2)], 5)
-
-    copy.wait()
+    loads[4].wait()
+    starts_copy.wait()
+    pos_copy.wait()
     for t in range(TILES):
-        at = pl.multiple_of(near[0, t] * 16, 16)
+        at = pl.multiple_of(starts_ref[0, t] * 16, 16)
         out_ref[2 * t] = blk[pl.ds(at, 16), :]
         out_ref[2 * t + 1] = blk[pl.ds(at + 16, 16), :]
 
@@ -152,10 +161,11 @@
     return pl.pallas_call(
         pack_kernel,
         in_specs=[pl.BlockSpec(memory_space=pltpu.HBM)] * 11,
+        out_specs=[pl.BlockSpec(memory_space=pltpu.SMEM if n in (1, 2) else pltpu.VMEM) for n in range(10)],
         out_shape=(
             jax.ShapeDtypeStruct((2 * TILES, 2 * FIELDS, LANES), F32),
-            jax.ShapeDtypeStruct((8, TILES), jnp.int32),
-            jax.ShapeDtypeStruct((8, TILES), jnp.int32),
+            pltpu.SMEM((8, TILES), jnp.int32),
+            pltpu.SMEM((8, TILES), jnp.int32),
             jax.ShapeDtypeStruct((ROWS // 2, LANES), F32),
             jax.ShapeDtypeStruct((ROWS // 2, LANES), F32),
         )
@@ -163,8 +173,9 @@
         scratch_shapes=[pltpu.VMEM(x.shape, x.dtype) for x in inputs[5:]]
         + [
             pltpu.VMEM(((SLOTS + 8) * 16, LANES), F32),
-            pltpu.SMEM((8, TILES), jnp.int32),
-            pltpu.SemaphoreType.DMA(()),
+            pltpu.VMEM((8, TILES), jnp.int32),
+            pltpu.VMEM((8, TILES), jnp.int32),
+            pltpu.SemaphoreType.DMA((2,)),
             pltpu.SemaphoreType.DMA((11,)),
         ],
         compiler_params=pltpu.CompilerParams(vmem_limit_bytes=VMEM_BYTES),
@@ -172,7 +183,7 @@
     )(*(pltpu.with_memory_space_constraint(x, pltpu.HBM) for x in inputs))
 
 
-def unpack_tile_kernel(pos_ref, recv_ref, temp_ref, sea_west_ref, sea_east_ref, tile_ref, west_ref, east_ref):
+def unpack_tile_kernel(pos_ref, recv_ref, temp_ref, sea_west_ref, sea_east_ref, tile_ref, west_ref, east_ref, room):
     chunk = lane_ids() // HALO
 
     def band(i):
@@ -185,7 +196,7 @@
                 got = recv_ref[pos_ref[0, k], h * FIELDS : (h + 1) * FIELDS, :]
                 four.append(jnp.where(pos_ref[1, k] > 0, got, 0.0))
             quads.append(four)
-        quads = yield from swap_chunks(quads)
+        quads = yield from swap_chunks(quads, room.at[i])
         for h in range(2):
             for r, x in enumerate(quads[h]):
                 tile_ref[pl.ds(base + h * 4 + r, FIELDS, stride=8), :] = x
@@ -207,7 +218,7 @@
         west_ref[rows, :] = west
         east_ref[rows, :] = east
 
-    interleave([band(i) for i in range(BANDS)], 5)
+    interleave([band(i) for i in range(BANDS)], 12)
     west_ref[ROWS:, :] = sea_west_ref[...]
     east_ref[ROWS:, :] = sea_east_ref[...]
 
@@ -224,6 +235,7 @@
             jax.ShapeDtypeStruct((EDGE, LANES), F32),
             jax.ShapeDtypeStruct((EDGE, LANES), F32),
         ),
+        scratch_shapes=[pltpu.VMEM((BANDS, 2, 4, 8, LANES), F32)],
         compiler_params=pltpu.CompilerParams(vmem_limit_bytes=VMEM_BYTES),
         name="unpack_tile",
     )(pos, recv, temp, sea_west, sea_east)
@@ -239,13 +251,13 @@
     here = slice(8 * i, 8 * i + 8)
     s["u"][at, :] = u
     s["v"][at, :] = v
-    s["p"][at, :] = cover * (total + diff)
-    s["m"][at, :] = cover * (total - diff)
-    s["t"][at, :] = cover * (shear + shear)
+    s["p"][at, :] = (0.25 * cover) * (total + diff)
+    s["m"][at, :] = (0.25 * cover) * (total - diff)
+    s["t"][at, :] = (0.5 * cover) * shear
     coriolis = 2.0 * (row_ids.astype(F32) + 0.5) / grid_rows - 1.0
     s["inertia"][here, :] = 2.0 * mass
     s["turn"][here, :] = mass * coriolis
-    s["k"][here, :] = (0.4 * I14) * (cover * strength)
+    s["k"][here, :] = (0.1 * I14) * (cover * strength)
     s["cover"][here, :] = cover
 
 
@@ -262,9 +274,9 @@
         s[name][8 + 8 * chunks : 16 + 8 * chunks, :] = zero
 
 
-def run_subcycles(s, chunks, times):
+def run_subcycles(s, stress_chunks, velocity_chunks, times=1):
     def subcycle(step, carry):
-        for i in chunks:
+        for i in stress_chunks:
             a = 8 + 8 * i
             at, up, down = slice(a, a + 8), slice(a + 1, a + 9), slice(a - 1, a + 7)
             here = slice(8 * i, 8 * i + 8)
@@ -274,21 +286,21 @@
             shear = (s["u"][up, :] - s["u"][down, :]) + (roll(v, -1) - roll(v, 1))
             div = exx + eyy
             ten = exx - eyy
-            q = div * div + 0.25 * (ten * ten + shear * shear) + 0.04
+            ten4, shear4 = 0.25 * ten, 0.25 * shear
+            q = div * div + (ten * ten4 + shear * shear4) + 0.04
             inv = lax.rsqrt(q)
             k = s["k"][here, :] * inv
             base = div - q * inv
-            ten = 0.25 * ten
-            s["p"][at, :] = I14 * s["p"][at, :] + k * (base + ten)
-            s["m"][at, :] = I14 * s["m"][at, :] + k * (base - ten)
-            s["t"][at, :] = I14 * s["t"][at, :] + (0.25 * k) * shear
-        for i in chunks:
+            s["p"][at, :] = I14 * s["p"][at, :] + k * (base + ten4)
+            s["m"][at, :] = I14 * s["m"][at, :] + k * (base - ten4)
+            s["t"][at, :] = I14 * s["t"][at, :] + k * shear4
+        for i in velocity_chunks:
             a = 8 + 8 * i
             at, up, down = slice(a, a + 8), slice(a + 1, a + 9), slice(a - 1, a + 7)
             here = slice(8 * i, 8 * i + 8)
             p, t = s["p"][at, :], s["t"][at, :]
-            fx = 0.25 * ((roll(p, -1) - roll(p, 1)) + (s["t"][up, :] - s["t"][down, :]))
-            fy = 0.25 * ((roll(t, -1) - roll(t, 1)) + (s["m"][up, :] - s["m"][down, :]))
+            fx = (roll(p, -1) - roll(p, 1)) + (s["t"][up, :] - s["t"][down, :])
+            fy = (roll(t, -1) - roll(t, 1)) + (s["m"][up, :] - s["m"][down, :])
             u, v = s["u"][at, :], s["v"][at, :]
             ou, ov = s["ou"][here, :], s["ov"][here, :]
             du, dv = ou - u, ov - v
@@ -303,7 +315,10 @@
             s["v"][at, :] = w * (diag * ry - turn * rx)
         return carry
 
-    lax.fori_loop(0, times, subcycle, 0)
+    if times == 1:
+        subcycle(0, 0)
+    else:
+        lax.fori_loop(0, times // 4, lambda n, c: [subcycle(n, c) for _ in range(4)][-1], 0)
 
 
 def state_scratch(chunks):
@@ -325,12 +340,12 @@
 
 
 def stresses(p, m, t):
-    return 0.5 * (p + m), 0.5 * (p - m), 0.5 * t
-
-
-def finals(s, i):
+    return 2.0 * (p + m), 2.0 * (p - m), 2.0 * t
+
+
+def state_of(s, i):
     at = slice(8 + 8 * i, 16 + 8 * i)
-    return [s["u"][at, :], s["v"][at, :], *stresses(s["p"][at, :], s["m"][at, :], s["t"][at, :])]
+    return [s[name][at, :] for name in STATE]
 
 
 def inner_kernel(tile_ref, ou_ref, ov_ref, wx_ref, wy_ref, out_ref, *scratch):
@@ -340,9 +355,9 @@
     for i in range(BANDS):
         put_ice(s, i, chunk_of(tile_ref, i), at_row(i), grid_rows)
         put_ocean(s, i, [ref[8 * i : 8 * i + 8, :] for ref in (ou_ref, ov_ref, wx_ref, wy_ref)])
-    run_subcycles(s, range(BANDS), SUBS)
+    run_subcycles(s, range(BANDS), range(BANDS), SUBS)
     for i in range(BANDS):
-        for f, x in enumerate(finals(s, i)):
+        for f, x in enumerate(state_of(s, i)):
             out_ref[f, 8 * i : 8 * i + 8, :] = x
 
 
@@ -396,23 +411,26 @@
     return jnp.where(lane >= LANES - HALO, moved, x)
 
 
-def finish_band(band, mids, strips, refs, stage, lane):
-    pos_ref, tile_ref, ou_ref, ov_ref, packed_ref, drag_ref = refs
-    moved = [roll(x, 32) for x in strips]
+def finish_band(band, mids, strips, refs, drag_ref, stage, room, lane):
+    pos_ref, tile_ref, ou_ref, ov_ref, packed_ref = refs
+    moved = [roll(x, 32) for x in strips()]
     yield
-    five = [join(*x, lane) for x in zip(mids, strips, moved)]
+    u, v, *pmt = [join(*x, lane) for x in zip(mids(), strips(), moved)]
+    five = [u, v, *stresses(*pmt)]
     for f, x in enumerate(five):
         for h in range(2):
-            at = h * FINAL * 4 + f * 4
+            at = h * 32 + f * 4
             stage[at : at + 4, :] = x[4 * h : 4 * h + 4, :]
     rows = slice(8 * band, 8 * band + 8)
     cover = tile_ref[band * 64 + 56 : band * 64 + 64, :]
-    drag_ref[0, rows, :], drag_ref[1, rows, :] = drag_rows(five, ou_ref[rows, :], ov_ref[rows, :], cover)
+    drag_ref[0], drag_ref[1] = drag_rows(five, ou_ref[rows, :], ov_ref[rows, :], cover)
     yield
-    quad = [stage[pl.ds(r, 2 * FINAL, stride=4), :] for r in range(4)]
-    (quad,) = yield from swap_chunks([quad])
-    for c, x in enumerate(quad):
-        packed_ref[pl.ds(pos_ref[0, band * 4 + c] * 2 * FINAL, 2 * FINAL), :] = x
+    quads = [[stage[pl.ds(32 * h + r, 8, stride=4), :] for r in range(4)] for h in range(2)]
+    quads = yield from swap_chunks(quads, room)
+    for c in range(4):
+        at = pos_ref[0, band * 4 + c] * 2 * FINAL
+        for h in range(2):
+            packed_ref[pl.ds(at + h * FINAL, FINAL), :] = quads[h][c][:FINAL]
 
 
 def drag_rows(five, ou, ov, cover):
@@ -423,7 +441,7 @@
 
 
 def sides_kernel(
-    pos_ref, tile_ref, west_ref, east_ref, ou_ref, ov_ref, wx_ref, wy_ref, mid_ref, packed_ref, drag_ref, stage, *scratch,
+    pos_ref, tile_ref, west_ref, east_ref, ou_ref, ov_ref, wx_ref, wy_ref, mid_ref, packed_ref, drag_ref, stage, room, *scratch,
 ):
     s = named(scratch)
     lane = lane_ids()
@@ -441,31 +459,33 @@
         put_ocean(s, i, (yield from ocean_strips(own, west_ref[sea, :], east_ref[sea, :], half, lane)))
 
     interleave([start(i) for i in range(BANDS)], 3)
-    run_subcycles(s, range(BANDS), SUBS)
-    refs = (pos_ref, tile_ref, ou_ref, ov_ref, packed_ref, drag_ref)
+    run_subcycles(s, range(BANDS), range(BANDS), SUBS)
+    refs = (pos_ref, tile_ref, ou_ref, ov_ref, packed_ref)
 
     def finish(i):
-        mids = [mid_ref[f, 8 * i : 8 * i + 8, :] for f in range(FINAL)]
-        yield from finish_band(i, mids, finals(s, i), refs, stage.at[i], lane)
-
-    interleave([finish(i) for i in range(2, BANDS - 2)], 6)
+        def mids():
+            return [mid_ref[f, 8 * i : 8 * i + 8, :] for f in range(FINAL)]
+
+        drag = drag_ref.at[:, pl.ds(8 * i - HALO, 8), :]
+        yield from finish_band(i, mids, lambda: state_of(s, i), refs, drag, stage.at[i], room.at[i], lane)
+
+    interleave([finish(i) for i in range(2, BANDS - 2)], 8)
 
 
 def stage_scratch(bands):
-    return [pltpu.VMEM((bands, 2 * FINAL * 4, LANES), F32)]
-
-
-RESULTS = (
-    jax.ShapeDtypeStruct((2 * TILES * 2 * FINAL, LANES), F32),
-    jax.ShapeDtypeStruct((2, ROWS, LANES), F32),
-)
+    return [pltpu.VMEM((bands, 64, LANES), F32), pltpu.VMEM((bands, 2, 4, 8, LANES), F32)]
+
+
+def results(rows):
+    return pltpu.VMEM((2 * TILES * 2 * FINAL, LANES), F32), jax.ShapeDtypeStruct((2, rows, LANES), F32)
 
 
 def sides(pos, tile, west, east, ocean, mid):
     return pl.pallas_call(
         sides_kernel,
         in_specs=specs(9),
-        out_shape=RESULTS,
+        out_shape=results(ROWS - 2 * HALO),
+        out_specs=specs(3)[1:],
         scratch_shapes=stage_scratch(BANDS) + state_scratch(BANDS),
         compiler_params=pltpu.CompilerParams(vmem_limit_bytes=VMEM_BYTES),
         cost_estimate=pl.CostEstimate(flops=5_000_000, bytes_accessed=5_000_000, transcendentals=800_000),
@@ -475,10 +495,9 @@
 
 def ends_kernel(
     pos_ref, tile_ref, west_ref, east_ref, north_ref, south_ref, ou_ref, ov_ref, wx_ref, wy_ref,
-    packed_in, drag_in, packed_ref, drag_ref, stage, *scratch,
+    packed_in, packed_ref, drag_ref, stage, room, *scratch,
 ):
-    packed_ref[...] = packed_in[...]
-    drag_ref[...] = drag_in[...]
+    del packed_in
     s = named(scratch)
     lane = lane_ids()
     grid_rows = ROWS * lax.axis_size("gy")
@@ -518,61 +537,93 @@
             put_ocean(s, chunk, water)
 
     interleave([start(end, j) for end in range(2) for j in range(6)], 3)
-    run_subcycles(s, range(24), SUBS // 2)
-    run_subcycles(s, [c for c in range(24) if c % 6 not in (0, 5)], SUBS // 2)
-    refs = (pos_ref, tile_ref, ou_ref, ov_ref, packed_ref, drag_ref)
+    every = range(24)
+    four = [c for c in every if c % 6 not in (0, 5)]
+    two = [c for c in every if c % 6 in (2, 3)]
+    for step in range(1, SUBS + 1):
+        stress = every if step < 5 else four
+        run_subcycles(s, stress, every if step < 4 else four if step < 8 else two)
+    refs = (pos_ref, tile_ref, ou_ref, ov_ref, packed_ref)
 
     def finish(n):
         end, j = divmod(n, 2)
         chunk = end * 6 + j + 2
         i = BANDS - 2 + j if end else j
-        yield from finish_band(i, finals(s, chunk), finals(s, chunk + 12), refs, stage.at[n], lane)
+        drag = drag_ref.at[:, pl.ds(8 * n, 8), :]
+        yield from finish_band(i, lambda: state_of(s, chunk), lambda: state_of(s, chunk + 12), refs, drag, stage.at[n], room.at[n], lane)
 
     interleave([finish(n) for n in range(4)], 4)
 
 
-def ends(pos, tile, west, east, north, south, ocean, packed, drag):
+def ends(pos, tile, west, east, north, south, ocean, packed):
+    packed = pltpu.with_memory_space_constraint(packed, pltpu.VMEM)
     return pl.pallas_call(
         ends_kernel,
-        in_specs=specs(12),
-        out_shape=RESULTS,
+        in_specs=specs(11),
+        out_shape=results(2 * HALO),
+        out_specs=specs(3)[1:],
+        input_output_aliases={10: 0},
         scratch_shapes=stage_scratch(4) + state_scratch(24),
         compiler_params=pltpu.CompilerParams(vmem_limit_bytes=VMEM_BYTES),
         name="ends",
-    )(pos, tile, west, east, north, south, *ocean, packed, drag)
-
-
-def unpack_ice_kernel(starts_ref, recv_ref, vel_ref, str_ref, blk):
+    )(pos, tile, west, east, north, south, *ocean, packed)
+
+
+def unpack_ice_kernel(starts_ref, recv_ref, mid_ref, end_ref, vel_out, str_out, drag_out, blk, vel_ref, str_ref, sems):
+    first, last = pl.ds(0, HALO), pl.ds(ROWS - HALO, HALO)
+    copies = [
+        pltpu.make_async_copy(mid_ref, drag_out.at[:, pl.ds(HALO, ROWS - 2 * HALO), :], sems.at[0]),
+        pltpu.make_async_copy(end_ref.at[:, first, :], drag_out.at[:, first, :], sems.at[1]),
+        pltpu.make_async_copy(end_ref.at[:, pl.ds(HALO, HALO), :], drag_out.at[:, last, :], sems.at[2]),
+    ]
+    for copy in copies:
+        copy.start()
     for t in range(TILES):
         start = starts_ref[0, t]
         for c in range(2):
             at = (2 * t + c) * 2 * FINAL
             to = pl.multiple_of((start + c) * 16, 16)
             blk[pl.ds(to, 2 * FINAL), :] = recv_ref[at : at + 2 * FINAL, :]
-    for g in range(SLOTS // 8):
-        eight = slice(8 * g, 8 * g + 8)
-        for h in range(2):
-            cut = slice(h * LANES, (h + 1) * LANES)
-            for f in range(3):
-                str_ref[f, eight, cut] = blk[pl.ds(128 * g + h * FINAL + 2 + f, 8, stride=16), :]
-            for j in range(8):
-                at = 128 * g + 16 * j + h * FINAL
-                vel_ref[8 * g + j, :, cut] = blk[at : at + 2, :]
-
-
-def unpack_ice(starts, recv):
-    vel, strs = pl.pallas_call(
+    half = SLOTS // 2
+    for part in range(2):
+        for g in range(part * half // 8, (part + 1) * half // 8):
+            eight = slice(8 * g, 8 * g + 8)
+            for h in range(2):
+                cut = slice(h * LANES, (h + 1) * LANES)
+                for f in range(3):
+                    str_ref[f, eight, cut] = blk[pl.ds(128 * g + h * FINAL + 2 + f, 8, stride=16), :]
+                for j in range(8):
+                    at = 128 * g + 16 * j + h * FINAL
+                    vel_ref[8 * g + j, :, cut] = blk[at : at + 2, :]
+        some = pl.ds(part * half, half)
+        parts = [
+            pltpu.make_async_copy(vel_ref.at[some], vel_out.at[some], sems.at[3 + 2 * part]),
+            pltpu.make_async_copy(str_ref.at[:, some, :], str_out.at[:, some, :], sems.at[4 + 2 * part]),
+        ]
+        for copy in parts:
+            copy.start()
+        copies += parts
+    for copy in copies:
+        copy.wait()
+
+
+def unpack_ice(starts, recv, drag_mid, drag_ends):
+    vel_shape, str_shape = (SLOTS, 2, 2 * LANES), (3, SLOTS, 2 * LANES)
+    vel, strs, drag = pl.pallas_call(
         unpack_ice_kernel,
-        in_specs=specs(2),
-        out_shape=(
-            jax.ShapeDtypeStruct((SLOTS, 2, 2 * LANES), F32),
-            jax.ShapeDtypeStruct((3, SLOTS, 2 * LANES), F32),
-        ),
-        scratch_shapes=[pltpu.VMEM(((SLOTS + 8) * 16, LANES), F32)],
+        in_specs=specs(4),
+        out_specs=[pl.BlockSpec(memory_space=pltpu.HBM)] * 3,
+        out_shape=tuple(pltpu.HBM(shape, F32) for shape in (vel_shape, str_shape, (2, ROWS, LANES))),
+        scratch_shapes=[
+            pltpu.VMEM(((SLOTS + 8) * 16, LANES), F32),
+            pltpu.VMEM(vel_shape, F32),
+            pltpu.VMEM(str_shape, F32),
+            pltpu.SemaphoreType.DMA((7,)),
+        ],
         compiler_params=pltpu.CompilerParams(vmem_limit_bytes=VMEM_BYTES),
         name="unpack_ice",
-    )(starts, recv)
-    return vel, jnp.transpose(strs, (1, 0, 2))
+    )(starts, recv, drag_mid, drag_ends)
+    return vel, jnp.transpose(strs, (1, 0, 2)), drag
 
 
 def both_ways(axis, forward, backward):
@@ -604,13 +655,12 @@
     low = edge(slice(0, HALO), slice(0, 128), slice(ROWS, ROWS + HALO))
     high = edge(slice(ROWS - HALO, ROWS), slice(-128, None), slice(EDGE - HALO, EDGE))
     north, south = both_ways("gy", high, low)
-    packed, drag = sides(pos, tile, west, east, ocean, mid)
-    packed, drag = ends(pos, tile, west, east, north, south, ocean, packed, drag)
+    packed, drag_mid = sides(pos, tile, west, east, ocean, mid)
+    packed, drag_ends = ends(pos, tile, west, east, north, south, ocean, packed)
 
     homeward = packed.reshape(2 * TILES, FINAL, 2, LANES)
     back = lax.all_to_all(homeward, AXES, split_axis=0, concat_axis=0, tiled=True)
-    vel, strs = unpack_ice(starts, back.reshape(2 * TILES * 2 * FINAL, LANES))
-    return vel, strs, drag
+    return unpack_ice(starts, back.reshape(2 * TILES * 2 * FINAL, LANES), drag_mid, drag_ends)
 
 
 def solution(mesh):

time: 101 us -> 95.8 us (0.949)
  Pallas kernels: 20.6 us -> 14.8 us
    pallas_call x3, Pallas kernels: 12.4 us -> 8.36 us  [the longest x1 4.87 us: sides(): pl.pallas_call(sides_kernel, in_specs=specs(9), out_shape=results(ROWS -...]
    pallas_call x1, Pallas kernels: 2.68 us -> 1.33 us  [unpack_tile(): pl.pallas_call(unpack_tile_kernel, in_specs=specs(5), out_shape=(jax.Shap...]
  transfers between devices with their start and end apart: 4 -> 4, of which waited for: 1 -> 1; matrix products, arithmetic and copies ran while one was open for 0% -> 0% of each run, Pallas kernels for 10% -> 8%
where the time goes in v2:
time: 95.8 us; the launch traced here: 95.6 us
  blocking collectives  72.1 us (75%)
  Pallas kernels  14.8 us (15%)
  starting transfers between devices  6.7 us (7%)
  waiting for transfers between devices  1.2 us (1%)
    all_to_all x1, blocking collectives, on_device(): lax.all_to_all(outbound, AXES, split_axis=0, concat_axis=0, tiled=True)  41.8 us
    all_to_all x1, blocking collectives, on_device(): lax.all_to_all(homeward, AXES, split_axis=0, concat_axis=0, tiled=True)  30.3 us
    ppermute x2, starting transfers between devices, both_ways(): lax.ppermute(backward, axis, [((i + 1) % n, i) for i in range(n)])  6.63 us
    pallas_call x1, Pallas kernels, sides(): pl.pallas_call(sides_kernel, in_specs=specs(9), out_shape=results(ROWS -...  4.87 us
    pallas_call x1, Pallas kernels, inner(): pl.pallas_call(inner_kernel, out_shape=jax.ShapeDtypeStruct((FINAL, ROWS,...  2.79 us
    pallas_call x1, Pallas kernels, ends(): pl.pallas_call(ends_kernel, in_specs=specs(11), out_shape=results(2 * HAL...  2.37 us
    pallas_call x1, Pallas kernels, pack(): pl.pallas_call(pack_kernel, in_specs=[pl.BlockSpec(memory_space=pltpu.HBM...  2.3 us
  transfers between devices with their start and end apart: 4, of which 1 were waited for; matrix products, arithmetic and copies ran while one was open for 0% of the time, Pallas kernels for 8%

profile of v2, /device:TPU:1, one launch (start us, length us, event | category | flops | bytes accessed | tf_op | source)
XLA Modules:
  0.0 95.6 jit_solution(14660970534830933947)
XLA Ops:
  0.6 2.3 %pack.1 = (f32[256,16,128]{2,1,0:T(8,128)S(1)}, s32[8,128]{1,0:T(8,128)S(4)}, s32[8,128]{1,0:T(8,128)S(4)}, f32[128,128]{1,0:T(8,128)S(1)}, f32[128,128]{1,0:T(8...) custom-call(f32[256,128]{1,0:T(8,128)} %refs_0_.1, ...), custom_call_target="tpu_custom_call" | custom-call | tf_op jit(solution)/shard_map/pack/pallas_call | solution.py:161
  2.9 41.8 %all_to_all.10.recv_ref = f32[256,16,128]{2,1,0:T(8,128)S(1)} all-to-all(f32[256,16,128]{2,1,0:T(8,128)S(1)} %get-tuple-element.28), channel_id=1, replica_groups=mesh['gx'=16,'gy'=8] {'gx','gy'}, dimensions={0} | all-to-all | bytes 4194304 | tf_op jit(solution)/shard_map/all_to_all | solution.py:645
  44.8 1.3 %unpack_tile.1 = (f32[2048,128]{1,0:T(8,128)S(1)}, f32[384,128]{1,0:T(8,128)S(1)}, f32[384,128]{1,0:T(8,128)S(1)}) custom-call(s32[8,128]{1,0:T(8,128)S(4)} %get-tuple-element.27.pos_ref, f32[256,16,128]{2,1,0:T(8,128)S(1)} %all_to_all.10.recv_ref, f32[256,128]{1,0:T(8,128)S(1)} %get-tuple-element.29.temp_ref, ...), custom_call_target="tpu_custom_call" | custom-call | tf_op jit(solution)/shard_map/unpack_tile/pallas_call | solution.py:230
  46.1 0.1 collective-permute-start
  46.2 4.8 %collective-permute-start.1 = (f32[384,128]{1,0:T(8,128)S(1)}, f32[384,128]{1,0:T(8,128)S(1)}, u32[]{:S(2)}, u32[]{:S(2)}) collective-permute-start(f32[384,128]{1,0:T(8,128)S(1)} %get-tuple-element.34), channel_id=1, source_target_pairs={{8,0},{16,8},{24,16},{32,24},{40,32},{48,40},{56,48},{64,56},{72,6... | collective-permute-start | bytes 589832 | tf_op jit(solution)/shard_map/ppermute | solution.py:633
  51.0 2.8 %inner.1.mid_ref = f32[5,256,128]{2,1,0:T(8,128)S(1)} custom-call(f32[2048,128]{1,0:T(8,128)S(1)} %get-tuple-element.32.tile_ref, f32[256,128]{1,0:T(8,128)S(1)} %get-tuple-element.35.ou_ref, f32[256,128]{1,0:T(8,128)S(1)} %get-tuple-element.36.ov_ref, f32[256,128]{1,0:T(8,128)S(1)} %get-tuple-element.37.wx_ref, f32[256,128]{1,0:T(8,128)S(1)} %get-tuple-element.38.wy_ref), custom_call_target="tpu_custom_call" | custom-call | flops 4000000 | bytes 4000000 | tf_op jit(solution)/shard_map/inner/pallas_call | solution.py:365
  53.8 1.2 %collective-permute-done.west_ref = f32[384,128]{1,0:T(8,128)S(1)} collective-permute-done((f32[384,128]{1,0:T(8,128)S(1)}, f32[384,128]{1,0:T(8,128)S(1)}, u32[]{:S(2)}, u32[]{:S(2)}) %collective-permute-start) | collective-permute-done | bytes 196640 | tf_op jit(solution)/shard_map/ppermute | solution.py:632
  55.0 0.0 collective-permute-done.1.east_ref
  55.1 1.9 %collective-permute-start.3 = (f32[256,128]{1,0:T(8,128)S(1)}, f32[256,128]{1,0:T(8,128)S(1)}, u32[]{:S(2)}, u32[]{:S(2)}) collective-permute-start(f32[256,128]{1,0:T(8,128)S(1)} %get-tuple-element.51), channel_id=1, source_target_pairs={{1,0},{2,1},{3,2},{4,3},{5,4},{6,5},{7,6},{0,7},{9,8},{10,9},{11,1... | collective-permute-start | bytes 393224 | tf_op jit(solution)/shard_map/ppermute | solution.py:633
  56.9 0.0 collective-permute-start.2
  56.9 4.9 %sides.1 = (f32[2560,128]{1,0:T(8,128)S(1)}, f32[2,224,128]{2,1,0:T(8,128)S(1)}) custom-call(s32[8,128]{1,0:T(8,128)S(4)} %get-tuple-element.27.pos_ref, f32[2048,128]{1,0:T(8,128)S(1)} %get-tuple-element.32.tile_ref, f32[384,128]{1,0:T(8,128)S(1)} %collective-permute-done.west_ref, f32[384,128]{1,0:T(8,128)S(1)} %collective-permute-done.1.east_ref, ...), custom_call_target="tpu_custom_call" | custom-call | flops 5000000 | bytes 5000000 | tf_op jit(solution)/shard_map/sides/pallas_call | solution.py:484
  61.8 0.0 collective-permute-done.3.south_ref
  61.8 0.0 collective-permute-done.2.north_ref
  61.8 2.4 %ends.1 = (f32[2560,128]{1,0:T(8,128)S(1)}, f32[2,32,128]{2,1,0:T(8,128)S(1)}) custom-call(s32[8,128]{1,0:T(8,128)S(4)} %get-tuple-element.27.pos_ref, f32[2048,128]{1,0:T(8,128)S(1)} %get-tuple-element.32.tile_ref, f32[384,128]{1,0:T(8,128)S(1)} %collective-permute-done.west_ref, ...), custom_call_target="tpu_custom_call", output_to_operand_aliasing={{0}: (10, {})} | custom-call | tf_op jit(solution)/shard_map/ends/pallas_call | solution.py:560
  64.2 30.3 %all_to_all.11 = f32[256,5,2,128]{3,2,1,0:T(2,128)S(1)} all-to-all(f32[256,5,2,128]{3,2,1,0:T(2,128)S(1)} %bitcast.6), channel_id=1, replica_groups=mesh['gx'=16,'gy'=8] {'gx','gy'}, dimensions={0} | all-to-all | bytes 2621440 | tf_op jit(solution)/shard_map/all_to_all | solution.py:662
  94.5 1.1 %unpack_ice.1 = (f32[112,2,256]{2,1,0:T(2,128)}, f32[3,112,256]{2,1,0:T(8,128)}, f32[2,256,128]{2,1,0:T(8,128)}) custom-call(s32[8,128]{1,0:T(8,128)S(4)} %get-tuple-element.26.starts_ref, f32[2560,128]{1,0:T(8,128)S(1)} %bitcast.7, f32[2,224,128]{2,1,0:T(8,128)S(1)} %get-tuple-element.44.mid_ref, f32[2,32,128]{2,1,0:T(8,128)S(1)} %get-tuple-element.45.end_ref), custom_call_target="tpu_custom_call" | custom-call | tf_op jit(solution)/shard_map/unpack_ice/pallas_call | solution.py:612
  (9 shorter events, 0.0 us)
Async XLA Ops:
  46.1 8.9 %collective-permute-start = (f32[384,128]{1,0:T(8,128)S(1)}, f32[384,128]{1,0:T(8,128)S(1)}, u32[]{:S(2)}, u32[]{:S(2)}) collective-permute-start(f32[384,128]{1,0:T(8,128)S(1)} %get-tuple-element.33), channel_id=1, source_target_pairs={{0,8},{8,16},{16,24},{24,32},{32,40},{40,48},{48,56},{56,64},{64,7... | collective-permute-start | bytes 589832 | tf_op jit(solution)/shard_map/ppermute | solution.py:632
  46.2 8.8 %collective-permute-start.1 = (f32[384,128]{1,0:T(8,128)S(1)}, f32[384,128]{1,0:T(8,128)S(1)}, u32[]{:S(2)}, u32[]{:S(2)}) collective-permute-start(f32[384,128]{1,0:T(8,128)S(1)} %get-tuple-element.34), channel_id=1, source_target_pairs={{8,0},{16,8},{24,16},{32,24},{40,32},{48,40},{56,48},{64,56},{72,6... | collective-permute-start | bytes 589832 | tf_op jit(solution)/shard_map/ppermute | solution.py:633
  55.1 6.7 %collective-permute-start.3 = (f32[256,128]{1,0:T(8,128)S(1)}, f32[256,128]{1,0:T(8,128)S(1)}, u32[]{:S(2)}, u32[]{:S(2)}) collective-permute-start(f32[256,128]{1,0:T(8,128)S(1)} %get-tuple-element.51), channel_id=1, source_target_pairs={{1,0},{2,1},{3,2},{4,3},{5,4},{6,5},{7,6},{0,7},{9,8},{10,9},{11,1... | collective-permute-start | bytes 393224 | tf_op jit(solution)/shard_map/ppermute | solution.py:633
  56.9 4.9 %collective-permute-start.2 = (f32[256,128]{1,0:T(8,128)S(1)}, f32[256,128]{1,0:T(8,128)S(1)}, u32[]{:S(2)}, u32[]{:S(2)}) collective-permute-start(f32[256,128]{1,0:T(8,128)S(1)} %get-tuple-element.52), channel_id=1, source_target_pairs={{0,1},{1,2},{2,3},{3,4},{4,5},{5,6},{6,7},{7,0},{8,9},{9,10},{10,1... | collective-permute-start | bytes 393224 | tf_op jit(solution)/shard_map/ppermute | solution.py:632

commit v3 on v2

--- a/solution.py
+++ b/solution.py
@@ -183,7 +183,13 @@
     )(*(pltpu.with_memory_space_constraint(x, pltpu.HBM) for x in inputs))
 
 
-def unpack_tile_kernel(pos_ref, recv_ref, temp_ref, sea_west_ref, sea_east_ref, tile_ref, west_ref, east_ref, room):
+def by_parity(axis, up, down):
+    even = lax.axis_index(axis) % 2 == 0
+    return jnp.where(even, up, down), jnp.where(even, down, up)
+
+
+def unpack_tile_kernel(pos_ref, recv_ref, temp_ref, sea_west_ref, sea_east_ref, tile_ref, near_ref, far_ref, even_ref, room):
+    even_ref[...] = by_parity("gy", jnp.ones((8, LANES), F32), jnp.zeros((8, LANES), F32))[0]
     chunk = lane_ids() // HALO
 
     def band(i):
@@ -215,12 +221,10 @@
         for f in range(1, FIELDS):
             west = jnp.where(chunk == f, moved[f], west)
             east = jnp.where(chunk == f - 1, moved[f], east)
-        west_ref[rows, :] = west
-        east_ref[rows, :] = east
+        near_ref[rows, :], far_ref[rows, :] = by_parity("gx", east, west)
 
     interleave([band(i) for i in range(BANDS)], 12)
-    west_ref[ROWS:, :] = sea_west_ref[...]
-    east_ref[ROWS:, :] = sea_east_ref[...]
+    near_ref[ROWS:, :], far_ref[ROWS:, :] = by_parity("gx", sea_east_ref[...], sea_west_ref[...])
 
 
 EDGE = ROWS + ROWS // 2
@@ -234,6 +238,7 @@
             jax.ShapeDtypeStruct((BANDS * FIELDS * 8, LANES), F32),
             jax.ShapeDtypeStruct((EDGE, LANES), F32),
             jax.ShapeDtypeStruct((EDGE, LANES), F32),
+            jax.ShapeDtypeStruct((8, LANES), F32),
         ),
         scratch_shapes=[pltpu.VMEM((BANDS, 2, 4, 8, LANES), F32)],
         compiler_params=pltpu.CompilerParams(vmem_limit_bytes=VMEM_BYTES),
@@ -441,7 +446,7 @@
 
 
 def sides_kernel(
-    pos_ref, tile_ref, west_ref, east_ref, ou_ref, ov_ref, wx_ref, wy_ref, mid_ref, packed_ref, drag_ref, stage, room, *scratch,
+    pos_ref, tile_ref, near_ref, far_ref, ou_ref, ov_ref, wx_ref, wy_ref, mid_ref, packed_ref, drag_ref, stage, room, *scratch,
 ):
     s = named(scratch)
     lane = lane_ids()
@@ -451,12 +456,14 @@
 
     def start(i):
         rows = slice(8 * i, 8 * i + 8)
-        ice = yield from ice_strips(chunk_of(tile_ref, i), west_ref[rows, :], east_ref[rows, :], edge, lane)
+        east, west = by_parity("gx", near_ref[rows, :], far_ref[rows, :])
+        ice = yield from ice_strips(chunk_of(tile_ref, i), west, east, edge, lane)
         put_ice(s, i, ice, at_row(i), grid_rows)
         half, j = divmod(i, BANDS // 2)
         sea = slice(ROWS + 8 * j, ROWS + 8 * j + 8)
         own = [ref[rows, :] for ref in (ou_ref, ov_ref, wx_ref, wy_ref)]
-        put_ocean(s, i, (yield from ocean_strips(own, west_ref[sea, :], east_ref[sea, :], half, lane)))
+        east, west = by_parity("gx", near_ref[sea, :], far_ref[sea, :])
+        put_ocean(s, i, (yield from ocean_strips(own, west, east, half, lane)))
 
     interleave([start(i) for i in range(BANDS)], 3)
     run_subcycles(s, range(BANDS), range(BANDS), SUBS)
@@ -494,7 +501,7 @@
 
 
 def ends_kernel(
-    pos_ref, tile_ref, west_ref, east_ref, north_ref, south_ref, ou_ref, ov_ref, wx_ref, wy_ref,
+    pos_ref, tile_ref, near_ref, far_ref, inner_ref, outer_ref, ou_ref, ov_ref, wx_ref, wy_ref,
     packed_in, packed_ref, drag_ref, stage, room, *scratch,
 ):
     del packed_in
@@ -507,27 +514,28 @@
     clear_ends(s, 24)
 
     def start(end, j):
-        ref = (north_ref, south_ref)[end]
         i = (j - 2) if end == 0 else BANDS - 4 + j
         half = 1 - end if not 0 <= i < BANDS else i // (BANDS // 2)
         if 0 <= i < BANDS:
             rows = slice(8 * i, 8 * i + 8)
             own = chunk_of(tile_ref, i)
-            west, east = west_ref[rows, :], east_ref[rows, :]
+            east, west = by_parity("gx", near_ref[rows, :], far_ref[rows, :])
             water = [x[rows, :] for x in ocean_refs]
             at = ROWS + 8 * (i % (BANDS // 2))
-            sea_west, sea_east = west_ref[at : at + 8, :], east_ref[at : at + 8, :]
+            sea_east, sea_west = by_parity("gx", near_ref[at : at + 8, :], far_ref[at : at + 8, :])
         else:
             at = 8 * (i % 2)
 
             def part_of(base):
-                return ref[base + at : base + at + 8, :]
-
-            own = [jnp.where(outside[end], 0.0, x) for x in chunk_of(ref, i % 2)]
-            west = jnp.where(outside[end], 0.0, part_of(128))
-            east = jnp.where(outside[end], 0.0, part_of(144))
-            water = [part_of(160 + 16 * f) for f in range(4)]
-            sea_west, sea_east = part_of(224), part_of(240)
+                rows = slice(base, base + 8)
+                south, north = by_parity("gy", inner_ref[rows, :], outer_ref[rows, :])
+                return south if end else north
+
+            own = [jnp.where(outside[end], 0.0, part_of(i % 2 * 64 + 8 * f)) for f in range(FIELDS)]
+            east, west = by_parity("gx", part_of(128 + at), part_of(144 + at))
+            west, east = jnp.where(outside[end], 0.0, west), jnp.where(outside[end], 0.0, east)
+            water = [part_of(160 + 16 * f + at) for f in range(4)]
+            sea_east, sea_west = by_parity("gx", part_of(224 + at), part_of(240 + at))
         for part in range(2):
             chunk = part * 12 + end * 6 + j
             ice = (yield from ice_strips(own, west, east, edge, lane)) if part else own
@@ -626,12 +634,19 @@
     return vel, jnp.transpose(strs, (1, 0, 2)), drag
 
 
-def both_ways(axis, forward, backward):
-    n = lax.axis_size(axis)
-    return (
-        lax.ppermute(forward, axis, [(i, (i + 1) % n) for i in range(n)]),
-        lax.ppermute(backward, axis, [((i + 1) % n, i) for i in range(n)]),
-    )
+def exchange(axis, near, far):
+    nx, ny = lax.axis_size("gx"), lax.axis_size("gy")
+    swaps = ([], [])
+    for a in range(nx):
+        for b in range(ny):
+            at, n = (a, nx) if axis == "gx" else (b, ny)
+            for swap, step in zip(swaps, (1 - at % 2 * 2, at % 2 * 2 - 1)):
+                to = (a + step, b) if axis == "gx" else (a, b + step)
+                if not 0 <= at + step < n:
+                    to = (a, b ^ 1) if axis == "gx" else (a ^ 1, b)
+                swap.append((a * ny + b, to[0] * ny + to[1]))
+    far = lax.ppermute(far, AXES, swaps[1])
+    return lax.ppermute(near, AXES, swaps[0]), far
 
 
 def on_device(
@@ -643,20 +658,21 @@
     )
     *ocean, surface_temp = maps
     arrived = lax.all_to_all(outbound, AXES, split_axis=0, concat_axis=0, tiled=True)
-    tile, west_edge, east_edge = unpack_tile(pos, arrived, surface_temp, sea_west, sea_east)
-    west, east = both_ways("gx", east_edge, west_edge)
-    west, east, mid = lax.optimization_barrier((west, east, inner(tile, ocean)))
+    tile, near, far, even = unpack_tile(pos, arrived, surface_temp, sea_west, sea_east)
+    near, far = exchange("gx", near, far)
+    near, far, mid, *ocean = lax.optimization_barrier((near, far, inner(tile, ocean), *ocean))
 
     def edge(cells, block_rows, sea_rows):
-        parts = [tile[block_rows], west[:ROWS][cells], east[:ROWS][cells]]
-        parts += [x[cells] for x in ocean] + [west[sea_rows], east[sea_rows]]
+        parts = [tile[block_rows], near[:ROWS][cells], far[:ROWS][cells]]
+        parts += [x[cells] for x in ocean] + [near[sea_rows], far[sea_rows]]
         return jnp.concatenate(parts, axis=0)
 
     low = edge(slice(0, HALO), slice(0, 128), slice(ROWS, ROWS + HALO))
     high = edge(slice(ROWS - HALO, ROWS), slice(-128, None), slice(EDGE - HALO, EDGE))
-    north, south = both_ways("gy", high, low)
-    packed, drag_mid = sides(pos, tile, west, east, ocean, mid)
-    packed, drag_ends = ends(pos, tile, west, east, north, south, ocean, packed)
+    even = even[:1] > 0.5
+    near_y, far_y = exchange("gy", jnp.where(even, high, low), jnp.where(even, low, high))
+    packed, drag_mid = sides(pos, tile, near, far, ocean, mid)
+    packed, drag_ends = ends(pos, tile, near, far, near_y, far_y, ocean, packed)
 
     homeward = packed.reshape(2 * TILES, FINAL, 2, LANES)
     back = lax.all_to_all(homeward, AXES, split_axis=0, concat_axis=0, tiled=True)

time: 95.8 us -> 91.1 us (0.951)
  blocking collectives: 72.1 us -> 68.9 us
  starting transfers between devices: 6.7 us -> 4.75 us
    all_to_all x1, blocking collectives: 30.3 us -> 27.1 us  [on_device(): lax.all_to_all(homeward, AXES, split_axis=0, concat_axis=0, tiled=True)]
    ppermute x4, starting transfers between devices: 6.7 us -> 4.75 us  [the longest x2 2.88 us: exchange(): far = lax.ppermute(far, AXES, swaps[1])]
where the time goes in v3:
time: 91.1 us; the launch traced here: 90.9 us
  blocking collectives  68.9 us (76%)
  Pallas kernels  14.8 us (16%)
  starting transfers between devices  4.75 us (5%)
  waiting for transfers between devices  1.63 us (2%)
    all_to_all x1, blocking collectives, on_device(): lax.all_to_all(outbound, AXES, split_axis=0, concat_axis=0, tiled=True)  41.8 us
    all_to_all x1, blocking collectives, on_device(): lax.all_to_all(homeward, AXES, split_axis=0, concat_axis=0, tiled=True)  27.1 us
    pallas_call x1, Pallas kernels, sides(): pl.pallas_call(sides_kernel, in_specs=specs(9), out_shape=results(ROWS -...  4.88 us
    ppermute x2, starting transfers between devices, exchange(): far = lax.ppermute(far, AXES, swaps[1])  2.88 us
    pallas_call x1, Pallas kernels, inner(): pl.pallas_call(inner_kernel, out_shape=jax.ShapeDtypeStruct((FINAL, ROWS,...  2.79 us
    pallas_call x1, Pallas kernels, ends(): pl.pallas_call(ends_kernel, in_specs=specs(11), out_shape=results(2 * HAL...  2.38 us
    pallas_call x1, Pallas kernels, pack(): pl.pallas_call(pack_kernel, in_specs=[pl.BlockSpec(memory_space=pltpu.HBM...  2.3 us
    ppermute x2, starting transfers between devices, exchange(): return (lax.ppermute(near, AXES, swaps[0]), far)  1.87 us
  transfers between devices with their start and end apart: 4, of which 1 were waited for; matrix products, arithmetic and copies ran while one was open for 0% of the time, Pallas kernels for 8%

profile of v3, /device:TPU:1, one launch (start us, length us, event | category | flops | bytes accessed | tf_op | source)
XLA Modules:
  0.0 90.9 jit_solution(3858368124839390943)
XLA Ops:
  0.6 2.3 %pack.1 = (f32[256,16,128]{2,1,0:T(8,128)S(1)}, s32[8,128]{1,0:T(8,128)S(4)}, s32[8,128]{1,0:T(8,128)S(4)}, f32[128,128]{1,0:T(8,128)S(1)}, f32[128,128]{1,0:T(8...) custom-call(f32[256,128]{1,0:T(8,128)} %refs_0_.1, ...), custom_call_target="tpu_custom_call" | custom-call | tf_op jit(solution)/shard_map/pack/pallas_call | solution.py:161
  2.9 41.8 %all_to_all.10.recv_ref = f32[256,16,128]{2,1,0:T(8,128)S(1)} all-to-all(f32[256,16,128]{2,1,0:T(8,128)S(1)} %get-tuple-element.33), channel_id=1, replica_groups=mesh['gx'=16,'gy'=8] {'gx','gy'}, dimensions={0} | all-to-all | bytes 4194304 | tf_op jit(solution)/shard_map/all_to_all | solution.py:660
  44.8 1.3 %unpack_tile.1 = (f32[2048,128]{1,0:T(8,128)S(1)}, f32[384,128]{1,0:T(8,128)S(1)}, f32[384,128]{1,0:T(8,128)S(1)}, f32[8,128]{1,0:T(8,128)S(1)}) custom-call(s32[8,128]{1,0:T(8,128)S(4)} %get-tuple-element.32.pos_ref, f32[256,16,128]{2,1,0:T(8,128)S(1)} %all_to_all.10.recv_ref, f32[256,128]{1,0:T(8,128)S(1)} %get-tuple-element.34.temp_ref, ...), custom_call_target="tpu_custom_call" | custom-call | tf_op jit(solution)/shard_map/unpack_tile/pallas_call | solution.py:234
  46.1 0.1 collective-permute-start
  46.2 1.0 %collective-permute-start.1 = (f32[384,128]{1,0:T(8,128)S(1)}, f32[384,128]{1,0:T(8,128)S(1)}, u32[]{:S(2)}, u32[]{:S(2)}) collective-permute-start(f32[384,128]{1,0:T(8,128)S(1)} %get-tuple-element.39), channel_id=1, source_target_pairs={{0,1},{1,0},{2,3},{3,2},{4,5},{5,4},{6,7},{7,6},{8,16},{9,17},{10,... | collective-permute-start | bytes 589832 | tf_op jit(solution)/shard_map/ppermute | solution.py:648
  47.2 2.8 %inner.1.mid_ref = f32[5,256,128]{2,1,0:T(8,128)S(1)} custom-call(f32[2048,128]{1,0:T(8,128)S(1)} %get-tuple-element.37.tile_ref, f32[256,128]{1,0:T(8,128)S(1)} %get-tuple-element.47.ou_ref, f32[256,128]{1,0:T(8,128)S(1)} %get-tuple-element.48.ov_ref, f32[256,128]{1,0:T(8,128)S(1)} %get-tuple-element.49.wx_ref, f32[256,128]{1,0:T(8,128)S(1)} %get-tuple-element.50.wy_ref), custom_call_target="tpu_custom_call" | custom-call | flops 4000000 | bytes 4000000 | tf_op jit(solution)/shard_map/inner/pallas_call | solution.py:370
  50.0 1.6 %collective-permute-done.near_ref = f32[384,128]{1,0:T(8,128)S(1)} collective-permute-done((f32[384,128]{1,0:T(8,128)S(1)}, f32[384,128]{1,0:T(8,128)S(1)}, u32[]{:S(2)}, u32[]{:S(2)}) %collective-permute-start) | collective-permute-done | bytes 196640 | tf_op jit(solution)/shard_map/ppermute | solution.py:649
  51.7 0.0 collective-permute-done.1.far_ref
  51.8 1.9 %collective-permute-start.3 = (f32[256,128]{1,0:T(8,128)S(1)}, f32[256,128]{1,0:T(8,128)S(1)}, u32[]{:S(2)}, u32[]{:S(2)}) collective-permute-start(f32[256,128]{1,0:T(8,128)S(1)} %get-tuple-element.61), channel_id=1, source_target_pairs={{0,8},{1,2},{2,1},{3,4},{4,3},{5,6},{6,5},{7,15},{8,0},{9,10},{10,... | collective-permute-start | bytes 393224 | tf_op jit(solution)/shard_map/ppermute | solution.py:648
  53.6 1.8 %collective-permute-start.2 = (f32[256,128]{1,0:T(8,128)S(1)}, f32[256,128]{1,0:T(8,128)S(1)}, u32[]{:S(2)}, u32[]{:S(2)}) collective-permute-start(f32[256,128]{1,0:T(8,128)S(1)} %get-tuple-element.62), channel_id=1, source_target_pairs={{0,1},{1,0},{2,3},{3,2},{4,5},{5,4},{6,7},{7,6},{8,9},{9,8},{10,11... | collective-permute-start | bytes 393224 | tf_op jit(solution)/shard_map/ppermute | solution.py:649
  55.4 4.9 %sides.1 = (f32[2560,128]{1,0:T(8,128)S(1)}, f32[2,224,128]{2,1,0:T(8,128)S(1)}) custom-call(s32[8,128]{1,0:T(8,128)S(4)} %get-tuple-element.32.pos_ref, f32[2048,128]{1,0:T(8,128)S(1)} %get-tuple-element.37.tile_ref, f32[384,128]{1,0:T(8,128)S(1)} %collective-permute-done.near_ref, f32[384,128]{1,0:T(8,128)S(1)} %collective-permute-done.1.far_ref, ...), custom_call_target="tpu_custom_call" | custom-call | flops 5000000 | bytes 5000000 | tf_op jit(solution)/shard_map/sides/pallas_call | solution.py:491
  60.3 0.0 collective-permute-done.3.outer_ref
  60.3 0.0 collective-permute-done.2.inner_ref
  60.3 2.4 %ends.1 = (f32[2560,128]{1,0:T(8,128)S(1)}, f32[2,32,128]{2,1,0:T(8,128)S(1)}) custom-call(s32[8,128]{1,0:T(8,128)S(4)} %get-tuple-element.32.pos_ref, f32[2048,128]{1,0:T(8,128)S(1)} %get-tuple-element.37.tile_ref, f32[384,128]{1,0:T(8,128)S(1)} %collective-permute-done.near_ref, ...), custom_call_target="tpu_custom_call", output_to_operand_aliasing={{0}: (10, {})} | custom-call | tf_op jit(solution)/shard_map/ends/pallas_call | solution.py:568
  62.7 27.1 %all_to_all.11 = f32[256,5,2,128]{3,2,1,0:T(2,128)S(1)} all-to-all(f32[256,5,2,128]{3,2,1,0:T(2,128)S(1)} %bitcast.8), channel_id=1, replica_groups=mesh['gx'=16,'gy'=8] {'gx','gy'}, dimensions={0} | all-to-all | bytes 2621440 | tf_op jit(solution)/shard_map/all_to_all | solution.py:678
  89.8 1.1 %unpack_ice.1 = (f32[112,2,256]{2,1,0:T(2,128)}, f32[3,112,256]{2,1,0:T(8,128)}, f32[2,256,128]{2,1,0:T(8,128)}) custom-call(s32[8,128]{1,0:T(8,128)S(4)} %get-tuple-element.31.starts_ref, f32[2560,128]{1,0:T(8,128)S(1)} %bitcast.9, f32[2,224,128]{2,1,0:T(8,128)S(1)} %get-tuple-element.54.mid_ref, f32[2,32,128]{2,1,0:T(8,128)S(1)} %get-tuple-element.55.end_ref), custom_call_target="tpu_custom_call" | custom-call | tf_op jit(solution)/shard_map/unpack_ice/pallas_call | solution.py:620
  (11 shorter events, 0.1 us)
Async XLA Ops:
  46.1 5.6 %collective-permute-start = (f32[384,128]{1,0:T(8,128)S(1)}, f32[384,128]{1,0:T(8,128)S(1)}, u32[]{:S(2)}, u32[]{:S(2)}) collective-permute-start(f32[384,128]{1,0:T(8,128)S(1)} %get-tuple-element.38), channel_id=1, source_target_pairs={{0,8},{1,9},{2,10},{3,11},{4,12},{5,13},{6,14},{7,15},{8,0},{9,1},... | collective-permute-start | bytes 589832 | tf_op jit(solution)/shard_map/ppermute | solution.py:649
  46.2 5.5 %collective-permute-start.1 = (f32[384,128]{1,0:T(8,128)S(1)}, f32[384,128]{1,0:T(8,128)S(1)}, u32[]{:S(2)}, u32[]{:S(2)}) collective-permute-start(f32[384,128]{1,0:T(8,128)S(1)} %get-tuple-element.39), channel_id=1, source_target_pairs={{0,1},{1,0},{2,3},{3,2},{4,5},{5,4},{6,7},{7,6},{8,16},{9,17},{10,... | collective-permute-start | bytes 589832 | tf_op jit(solution)/shard_map/ppermute | solution.py:648
  51.8 8.5 %collective-permute-start.3 = (f32[256,128]{1,0:T(8,128)S(1)}, f32[256,128]{1,0:T(8,128)S(1)}, u32[]{:S(2)}, u32[]{:S(2)}) collective-permute-start(f32[256,128]{1,0:T(8,128)S(1)} %get-tuple-element.61), channel_id=1, source_target_pairs={{0,8},{1,2},{2,1},{3,4},{4,3},{5,6},{6,5},{7,15},{8,0},{9,10},{10,... | collective-permute-start | bytes 393224 | tf_op jit(solution)/shard_map/ppermute | solution.py:648
  53.6 6.7 %collective-permute-start.2 = (f32[256,128]{1,0:T(8,128)S(1)}, f32[256,128]{1,0:T(8,128)S(1)}, u32[]{:S(2)}, u32[]{:S(2)}) collective-permute-start(f32[256,128]{1,0:T(8,128)S(1)} %get-tuple-element.62), channel_id=1, source_target_pairs={{0,1},{1,0},{2,3},{3,2},{4,5},{5,4},{6,7},{7,6},{8,9},{9,8},{10,11... | collective-permute-start | bytes 393224 | tf_op jit(solution)/shard_map/ppermute | solution.py:649

commit v4 on v3

--- a/solution.py
+++ b/solution.py
@@ -121,6 +121,8 @@
             west = jnp.where(chunk == n, moved[n], west)
             east = jnp.where(chunk == n - 1, moved[n], east)
         west_ref[8 * i : 8 * i + 8, :] = west
+        east = roll(east, 2 * HALO)
+        yield
         east_ref[8 * i : 8 * i + 8, :] = east
 
     interleave([sea_edges(i) for i in range(BANDS // 2)], 5)
@@ -188,7 +190,7 @@
     return jnp.where(even, up, down), jnp.where(even, down, up)
 
 
-def unpack_tile_kernel(pos_ref, recv_ref, temp_ref, sea_west_ref, sea_east_ref, tile_ref, near_ref, far_ref, even_ref, room):
+def unpack_tile_kernel(pos_ref, recv_ref, temp_ref, sea_west_ref, sea_east_ref, tile_ref, near_ref, far_ref, even_ref, room, edges):
     even_ref[...] = by_parity("gy", jnp.ones((8, LANES), F32), jnp.zeros((8, LANES), F32))[0]
     chunk = lane_ids() // HALO
 
@@ -221,9 +223,17 @@
         for f in range(1, FIELDS):
             west = jnp.where(chunk == f, moved[f], west)
             east = jnp.where(chunk == f - 1, moved[f], east)
-        near_ref[rows, :], far_ref[rows, :] = by_parity("gx", east, west)
+        edges[0, rows, :] = west
+        edges[1, rows, :] = east
+
+    def edge(i):
+        rows = slice(8 * i, 8 * i + 8)
+        east = roll(edges[1, rows, :], 2 * HALO)
+        yield
+        near_ref[rows, :], far_ref[rows, :] = by_parity("gx", east, edges[0, rows, :])
 
     interleave([band(i) for i in range(BANDS)], 12)
+    interleave([edge(i) for i in range(BANDS)], 16)
     near_ref[ROWS:, :], far_ref[ROWS:, :] = by_parity("gx", sea_east_ref[...], sea_west_ref[...])
 
 
@@ -240,7 +250,7 @@
             jax.ShapeDtypeStruct((EDGE, LANES), F32),
             jax.ShapeDtypeStruct((8, LANES), F32),
         ),
-        scratch_shapes=[pltpu.VMEM((BANDS, 2, 4, 8, LANES), F32)],
+        scratch_shapes=[pltpu.VMEM((BANDS, 2, 4, 8, LANES), F32), pltpu.VMEM((2, ROWS, LANES), F32)],
         compiler_params=pltpu.CompilerParams(vmem_limit_bytes=VMEM_BYTES),
         name="unpack_tile",
     )(pos, recv, temp, sea_west, sea_east)
@@ -377,26 +387,25 @@
     )(tile, *ocean)
 
 
-def strip_moves(own, west, east, chunk):
-    return own, roll(own, -32), roll(west, (8 - chunk) * HALO), roll(east, (6 - chunk) * HALO)
-
-
-def strip(own, moved, west, east, lane):
-    x = jnp.where(lane < 48, own, moved)
-    x = jnp.where(lane >= 112, west, x)
-    return jnp.where((lane >= 96) & (lane < 112), east, x)
+def strip_moves(own, west, east, n, lane):
+    halo = jnp.where(lane // HALO == n, east, west)
+    return own, roll(own, -32), roll(halo, (6 - n) * HALO)
+
+
+def strip(own, moved, halo, lane):
+    return jnp.where(lane >= 96, halo, jnp.where(lane < 48, own, moved))
 
 
 def ice_strips(own, west, east, edge, lane):
     west = jnp.where(edge[0], 0.0, west)
     east = jnp.where(edge[1], 0.0, east)
-    moved = [strip_moves(own[f], west, east, f) for f in range(FIELDS)]
+    moved = [strip_moves(own[f], west, east, f, lane) for f in range(FIELDS)]
     yield
     return [strip(*x, lane) for x in moved]
 
 
 def ocean_strips(own, west, east, half, lane):
-    moved = [strip_moves(own[f], west, east, 4 * half + f) for f in range(4)]
+    moved = [strip_moves(own[f], west, east, 4 * half + f, lane) for f in range(4)]
     yield
     return [strip(*x, lane) for x in moved]
 

time: 91.1 us -> 90.6 us (level)
  no operation moved by 1% of the time
where the time goes in v4:
time: 90.6 us; the launch traced here: 90.5 us
  blocking collectives  68.9 us (76%)
  Pallas kernels  14.4 us (16%)
  starting transfers between devices  4.75 us (5%)
  waiting for transfers between devices  1.63 us (2%)
    all_to_all x1, blocking collectives, on_device(): lax.all_to_all(outbound, AXES, split_axis=0, concat_axis=0, tiled=True)  41.8 us
    all_to_all x1, blocking collectives, on_device(): lax.all_to_all(homeward, AXES, split_axis=0, concat_axis=0, tiled=True)  27.1 us
    pallas_call x1, Pallas kernels, sides(): pl.pallas_call(sides_kernel, in_specs=specs(9), out_shape=results(ROWS -...  4.52 us
    ppermute x2, starting transfers between devices, exchange(): far = lax.ppermute(far, AXES, swaps[1])  2.88 us
    pallas_call x1, Pallas kernels, inner(): pl.pallas_call(inner_kernel, out_shape=jax.ShapeDtypeStruct((FINAL, ROWS,...  2.79 us
    pallas_call x1, Pallas kernels, pack(): pl.pallas_call(pack_kernel, in_specs=[pl.BlockSpec(memory_space=pltpu.HBM...  2.3 us
    pallas_call x1, Pallas kernels, ends(): pl.pallas_call(ends_kernel, in_specs=specs(11), out_shape=results(2 * HAL...  2.24 us
    ppermute x2, starting transfers between devices, exchange(): return (lax.ppermute(near, AXES, swaps[0]), far)  1.87 us
  transfers between devices with their start and end apart: 4, of which 1 were waited for; matrix products, arithmetic and copies ran while one was open for 0% of the time, Pallas kernels for 8%

profile of v4, /device:TPU:1, one launch (start us, length us, event | category | flops | bytes accessed | tf_op | source)
XLA Modules:
  0.0 90.5 jit_solution(7717193182364527597)
XLA Ops:
  0.6 2.3 %pack.1 = (f32[256,16,128]{2,1,0:T(8,128)S(1)}, s32[8,128]{1,0:T(8,128)S(4)}, s32[8,128]{1,0:T(8,128)S(4)}, f32[128,128]{1,0:T(8,128)S(1)}, f32[128,128]{1,0:T(8...) custom-call(f32[256,128]{1,0:T(8,128)} %refs_0_.1, ...), custom_call_target="tpu_custom_call" | custom-call | tf_op jit(solution)/shard_map/pack/pallas_call | solution.py:163
  2.9 41.8 %all_to_all.10.recv_ref = f32[256,16,128]{2,1,0:T(8,128)S(1)} all-to-all(f32[256,16,128]{2,1,0:T(8,128)S(1)} %get-tuple-element.33), channel_id=1, replica_groups=mesh['gx'=16,'gy'=8] {'gx','gy'}, dimensions={0} | all-to-all | bytes 4194304 | tf_op jit(solution)/shard_map/all_to_all | solution.py:669
  44.8 1.4 %unpack_tile.1 = (f32[2048,128]{1,0:T(8,128)S(1)}, f32[384,128]{1,0:T(8,128)S(1)}, f32[384,128]{1,0:T(8,128)S(1)}, f32[8,128]{1,0:T(8,128)S(1)}) custom-call(s32[8,128]{1,0:T(8,128)S(4)} %get-tuple-element.32.pos_ref, f32[256,16,128]{2,1,0:T(8,128)S(1)} %all_to_all.10.recv_ref, f32[256,128]{1,0:T(8,128)S(1)} %get-tuple-element.34.temp_ref, ...), custom_call_target="tpu_custom_call" | custom-call | tf_op jit(solution)/shard_map/unpack_tile/pallas_call | solution.py:244
  46.2 0.1 collective-permute-start
  46.3 1.0 %collective-permute-start.1 = (f32[384,128]{1,0:T(8,128)S(1)}, f32[384,128]{1,0:T(8,128)S(1)}, u32[]{:S(2)}, u32[]{:S(2)}) collective-permute-start(f32[384,128]{1,0:T(8,128)S(1)} %get-tuple-element.39), channel_id=1, source_target_pairs={{0,1},{1,0},{2,3},{3,2},{4,5},{5,4},{6,7},{7,6},{8,16},{9,17},{10,... | collective-permute-start | bytes 589832 | tf_op jit(solution)/shard_map/ppermute | solution.py:657
  47.3 2.8 %inner.1.mid_ref = f32[5,256,128]{2,1,0:T(8,128)S(1)} custom-call(f32[2048,128]{1,0:T(8,128)S(1)} %get-tuple-element.37.tile_ref, f32[256,128]{1,0:T(8,128)S(1)} %get-tuple-element.47.ou_ref, f32[256,128]{1,0:T(8,128)S(1)} %get-tuple-element.48.ov_ref, f32[256,128]{1,0:T(8,128)S(1)} %get-tuple-element.49.wx_ref, f32[256,128]{1,0:T(8,128)S(1)} %get-tuple-element.50.wy_ref), custom_call_target="tpu_custom_call" | custom-call | flops 4000000 | bytes 4000000 | tf_op jit(solution)/shard_map/inner/pallas_call | solution.py:380
  50.1 1.6 %collective-permute-done.near_ref = f32[384,128]{1,0:T(8,128)S(1)} collective-permute-done((f32[384,128]{1,0:T(8,128)S(1)}, f32[384,128]{1,0:T(8,128)S(1)}, u32[]{:S(2)}, u32[]{:S(2)}) %collective-permute-start) | collective-permute-done | bytes 196640 | tf_op jit(solution)/shard_map/ppermute | solution.py:658
  51.7 0.0 collective-permute-done.1.far_ref
  51.8 1.9 %collective-permute-start.3 = (f32[256,128]{1,0:T(8,128)S(1)}, f32[256,128]{1,0:T(8,128)S(1)}, u32[]{:S(2)}, u32[]{:S(2)}) collective-permute-start(f32[256,128]{1,0:T(8,128)S(1)} %get-tuple-element.61), channel_id=1, source_target_pairs={{0,8},{1,2},{2,1},{3,4},{4,3},{5,6},{6,5},{7,15},{8,0},{9,10},{10,... | collective-permute-start | bytes 393224 | tf_op jit(solution)/shard_map/ppermute | solution.py:657
  53.7 1.8 %collective-permute-start.2 = (f32[256,128]{1,0:T(8,128)S(1)}, f32[256,128]{1,0:T(8,128)S(1)}, u32[]{:S(2)}, u32[]{:S(2)}) collective-permute-start(f32[256,128]{1,0:T(8,128)S(1)} %get-tuple-element.62), channel_id=1, source_target_pairs={{0,1},{1,0},{2,3},{3,2},{4,5},{5,4},{6,7},{7,6},{8,9},{9,8},{10,11... | collective-permute-start | bytes 393224 | tf_op jit(solution)/shard_map/ppermute | solution.py:658
  55.5 4.5 %sides.1 = (f32[2560,128]{1,0:T(8,128)S(1)}, f32[2,224,128]{2,1,0:T(8,128)S(1)}) custom-call(s32[8,128]{1,0:T(8,128)S(4)} %get-tuple-element.32.pos_ref, f32[2048,128]{1,0:T(8,128)S(1)} %get-tuple-element.37.tile_ref, f32[384,128]{1,0:T(8,128)S(1)} %collective-permute-done.near_ref, f32[384,128]{1,0:T(8,128)S(1)} %collective-permute-done.1.far_ref, ...), custom_call_target="tpu_custom_call" | custom-call | flops 5000000 | bytes 5000000 | tf_op jit(solution)/shard_map/sides/pallas_call | solution.py:500
  60.0 0.0 collective-permute-done.3.outer_ref
  60.0 0.0 collective-permute-done.2.inner_ref
  60.0 2.2 %ends.1 = (f32[2560,128]{1,0:T(8,128)S(1)}, f32[2,32,128]{2,1,0:T(8,128)S(1)}) custom-call(s32[8,128]{1,0:T(8,128)S(4)} %get-tuple-element.32.pos_ref, f32[2048,128]{1,0:T(8,128)S(1)} %get-tuple-element.37.tile_ref, f32[384,128]{1,0:T(8,128)S(1)} %collective-permute-done.near_ref, ...), custom_call_target="tpu_custom_call", output_to_operand_aliasing={{0}: (10, {})} | custom-call | tf_op jit(solution)/shard_map/ends/pallas_call | solution.py:577
  62.3 27.1 %all_to_all.11 = f32[256,5,2,128]{3,2,1,0:T(2,128)S(1)} all-to-all(f32[256,5,2,128]{3,2,1,0:T(2,128)S(1)} %bitcast.8), channel_id=1, replica_groups=mesh['gx'=16,'gy'=8] {'gx','gy'}, dimensions={0} | all-to-all | bytes 2621440 | tf_op jit(solution)/shard_map/all_to_all | solution.py:687
  89.3 1.1 %unpack_ice.1 = (f32[112,2,256]{2,1,0:T(2,128)}, f32[3,112,256]{2,1,0:T(8,128)}, f32[2,256,128]{2,1,0:T(8,128)}) custom-call(s32[8,128]{1,0:T(8,128)S(4)} %get-tuple-element.31.starts_ref, f32[2560,128]{1,0:T(8,128)S(1)} %bitcast.9, f32[2,224,128]{2,1,0:T(8,128)S(1)} %get-tuple-element.54.mid_ref, f32[2,32,128]{2,1,0:T(8,128)S(1)} %get-tuple-element.55.end_ref), custom_call_target="tpu_custom_call" | custom-call | tf_op jit(solution)/shard_map/unpack_ice/pallas_call | solution.py:629
  (11 shorter events, 0.1 us)
Async XLA Ops:
  46.2 5.6 %collective-permute-start = (f32[384,128]{1,0:T(8,128)S(1)}, f32[384,128]{1,0:T(8,128)S(1)}, u32[]{:S(2)}, u32[]{:S(2)}) collective-permute-start(f32[384,128]{1,0:T(8,128)S(1)} %get-tuple-element.38), channel_id=1, source_target_pairs={{0,8},{1,9},{2,10},{3,11},{4,12},{5,13},{6,14},{7,15},{8,0},{9,1},... | collective-permute-start | bytes 589832 | tf_op jit(solution)/shard_map/ppermute | solution.py:658
  46.3 5.5 %collective-permute-start.1 = (f32[384,128]{1,0:T(8,128)S(1)}, f32[384,128]{1,0:T(8,128)S(1)}, u32[]{:S(2)}, u32[]{:S(2)}) collective-permute-start(f32[384,128]{1,0:T(8,128)S(1)} %get-tuple-element.39), channel_id=1, source_target_pairs={{0,1},{1,0},{2,3},{3,2},{4,5},{5,4},{6,7},{7,6},{8,16},{9,17},{10,... | collective-permute-start | bytes 589832 | tf_op jit(solution)/shard_map/ppermute | solution.py:657
  51.8 8.2 %collective-permute-start.3 = (f32[256,128]{1,0:T(8,128)S(1)}, f32[256,128]{1,0:T(8,128)S(1)}, u32[]{:S(2)}, u32[]{:S(2)}) collective-permute-start(f32[256,128]{1,0:T(8,128)S(1)} %get-tuple-element.61), channel_id=1, source_target_pairs={{0,8},{1,2},{2,1},{3,4},{4,3},{5,6},{6,5},{7,15},{8,0},{9,10},{10,... | collective-permute-start | bytes 393224 | tf_op jit(solution)/shard_map/ppermute | solution.py:657
  53.7 6.3 %collective-permute-start.2 = (f32[256,128]{1,0:T(8,128)S(1)}, f32[256,128]{1,0:T(8,128)S(1)}, u32[]{:S(2)}, u32[]{:S(2)}) collective-permute-start(f32[256,128]{1,0:T(8,128)S(1)} %get-tuple-element.62), channel_id=1, source_target_pairs={{0,1},{1,0},{2,3},{3,2},{4,5},{5,4},{6,7},{7,6},{8,9},{9,8},{10,11... | collective-permute-start | bytes 393224 | tf_op jit(solution)/shard_map/ppermute | solution.py:658

commit v5 on v4

--- a/solution.py
+++ b/solution.py
@@ -76,7 +76,7 @@
     here, (blk, starts_v, pos_v, scalars, sems) = refs[:11], refs[11:]
     ou_ref, ov_ref, wx_ref, wy_ref, _, owner_ref, con_ref, thk_ref, str_ref, mask_ref, vel_ref = here
     loads = [pltpu.make_async_copy(x, y, sems.at[n]) for n, (x, y) in enumerate(zip(far, here))]
-    for n in (5, 0, 1, 2, 3, 6, 7, 8, 9, 10, 4):
+    for n in (5, 6, 7, 8, 9, 10, 0, 1, 2, 3, 4):
         loads[n].start()
     loads[5].wait()
     me = lax.axis_index("gx") * lax.axis_size("gy") + lax.axis_index("gy")
@@ -104,28 +104,6 @@
     pos_v[...] = jnp.where(row == 0, slot, jnp.where(icy, 1.0, 0.0)).astype(jnp.int32)
     pos_copy = pltpu.make_async_copy(pos_v, pos_ref, scalars.at[1])
     pos_copy.start()
-
-    for n in range(4):
-        loads[n].wait()
-    chunk = lane_ids() // HALO
-
-    def sea_edges(i):
-        moved = []
-        for half in range(2):
-            rows = slice(8 * i + half * LANES, 8 * i + half * LANES + 8)
-            for f, ref in enumerate((ou_ref, ov_ref, wx_ref, wy_ref)):
-                moved.append(roll(ref[rows, :], (4 * half + f) * HALO))
-        yield
-        west, east = moved[0], moved[0]
-        for n in range(1, 8):
-            west = jnp.where(chunk == n, moved[n], west)
-            east = jnp.where(chunk == n - 1, moved[n], east)
-        west_ref[8 * i : 8 * i + 8, :] = west
-        east = roll(east, 2 * HALO)
-        yield
-        east_ref[8 * i : 8 * i + 8, :] = east
-
-    interleave([sea_edges(i) for i in range(BANDS // 2)], 5)
 
     for n in range(6, 11):
         loads[n].wait()
@@ -144,13 +122,35 @@
                 at = 128 * g + 16 * j + 8 * h
                 blk[at : at + 2, :] = vel_ref[8 * g + j, :, cut]
 
-    loads[4].wait()
     starts_copy.wait()
-    pos_copy.wait()
     for t in range(TILES):
         at = pl.multiple_of(starts_ref[0, t] * 16, 16)
         out_ref[2 * t] = blk[pl.ds(at, 16), :]
         out_ref[2 * t + 1] = blk[pl.ds(at + 16, 16), :]
+
+    for n in range(4):
+        loads[n].wait()
+    chunk = lane_ids() // HALO
+
+    def sea_edges(i):
+        moved = []
+        for half in range(2):
+            rows = slice(8 * i + half * LANES, 8 * i + half * LANES + 8)
+            for f, ref in enumerate((ou_ref, ov_ref, wx_ref, wy_ref)):
+                moved.append(roll(ref[rows, :], (4 * half + f) * HALO))
+        yield
+        west, east = moved[0], moved[0]
+        for n in range(1, 8):
+            west = jnp.where(chunk == n, moved[n], west)
+            east = jnp.where(chunk == n - 1, moved[n], east)
+        west_ref[8 * i : 8 * i + 8, :] = west
+        east = roll(east, 2 * HALO)
+        yield
+        east_ref[8 * i : 8 * i + 8, :] = east
+
+    interleave([sea_edges(i) for i in range(BANDS // 2)], 5)
+    loads[4].wait()
+    pos_copy.wait()
 
 
 def pack(owner_list, ice_mask, velocity, stress, thickness, concentration, maps):

time: 90.6 us -> 90.7 us (level)
  no operation moved by 1% of the time
where the time goes in v5:
time: 90.7 us; the launch traced here: 90.5 us
  blocking collectives  68.9 us (76%)
  Pallas kernels  14.4 us (16%)
  starting transfers between devices  4.75 us (5%)
  waiting for transfers between devices  1.63 us (2%)
    all_to_all x1, blocking collectives, on_device(): lax.all_to_all(outbound, AXES, split_axis=0, concat_axis=0, tiled=True)  41.8 us
    all_to_all x1, blocking collectives, on_device(): lax.all_to_all(homeward, AXES, split_axis=0, concat_axis=0, tiled=True)  27.1 us
    pallas_call x1, Pallas kernels, sides(): pl.pallas_call(sides_kernel, in_specs=specs(9), out_shape=results(ROWS -...  4.52 us
    ppermute x2, starting transfers between devices, exchange(): far = lax.ppermute(far, AXES, swaps[1])  2.88 us
    pallas_call x1, Pallas kernels, inner(): pl.pallas_call(inner_kernel, out_shape=jax.ShapeDtypeStruct((FINAL, ROWS,...  2.79 us
    pallas_call x1, Pallas kernels, pack(): pl.pallas_call(pack_kernel, in_specs=[pl.BlockSpec(memory_space=pltpu.HBM...  2.37 us
    pallas_call x1, Pallas kernels, ends(): pl.pallas_call(ends_kernel, in_specs=specs(11), out_shape=results(2 * HAL...  2.24 us
    ppermute x2, starting transfers between devices, exchange(): return (lax.ppermute(near, AXES, swaps[0]), far)  1.87 us
  transfers between devices with their start and end apart: 4, of which 1 were waited for; matrix products, arithmetic and copies ran while one was open for 0% of the time, Pallas kernels for 8%

profile of v5, /device:TPU:1, one launch (start us, length us, event | category | flops | bytes accessed | tf_op | source)
XLA Modules:
  0.0 90.5 jit_solution(15598478671629171078)
XLA Ops:
  0.6 2.4 %pack.1 = (f32[256,16,128]{2,1,0:T(8,128)S(1)}, s32[8,128]{1,0:T(8,128)S(4)}, s32[8,128]{1,0:T(8,128)S(4)}, f32[128,128]{1,0:T(8,128)S(1)}, f32[128,128]{1,0:T(8...) custom-call(f32[256,128]{1,0:T(8,128)} %refs_0_.1, ...), custom_call_target="tpu_custom_call" | custom-call | tf_op jit(solution)/shard_map/pack/pallas_call | solution.py:163
  3.0 41.8 %all_to_all.10.recv_ref = f32[256,16,128]{2,1,0:T(8,128)S(1)} all-to-all(f32[256,16,128]{2,1,0:T(8,128)S(1)} %get-tuple-element.33), channel_id=1, replica_groups=mesh['gx'=16,'gy'=8] {'gx','gy'}, dimensions={0} | all-to-all | bytes 4194304 | tf_op jit(solution)/shard_map/all_to_all | solution.py:669
  44.8 1.4 %unpack_tile.1 = (f32[2048,128]{1,0:T(8,128)S(1)}, f32[384,128]{1,0:T(8,128)S(1)}, f32[384,128]{1,0:T(8,128)S(1)}, f32[8,128]{1,0:T(8,128)S(1)}) custom-call(s32[8,128]{1,0:T(8,128)S(4)} %get-tuple-element.32.pos_ref, f32[256,16,128]{2,1,0:T(8,128)S(1)} %all_to_all.10.recv_ref, f32[256,128]{1,0:T(8,128)S(1)} %get-tuple-element.34.temp_ref, ...), custom_call_target="tpu_custom_call" | custom-call | tf_op jit(solution)/shard_map/unpack_tile/pallas_call | solution.py:244
  46.2 0.1 collective-permute-start
  46.3 1.0 %collective-permute-start.1 = (f32[384,128]{1,0:T(8,128)S(1)}, f32[384,128]{1,0:T(8,128)S(1)}, u32[]{:S(2)}, u32[]{:S(2)}) collective-permute-start(f32[384,128]{1,0:T(8,128)S(1)} %get-tuple-element.39), channel_id=1, source_target_pairs={{0,1},{1,0},{2,3},{3,2},{4,5},{5,4},{6,7},{7,6},{8,16},{9,17},{10,... | collective-permute-start | bytes 589832 | tf_op jit(solution)/shard_map/ppermute | solution.py:657
  47.3 2.8 %inner.1.mid_ref = f32[5,256,128]{2,1,0:T(8,128)S(1)} custom-call(f32[2048,128]{1,0:T(8,128)S(1)} %get-tuple-element.37.tile_ref, f32[256,128]{1,0:T(8,128)S(1)} %get-tuple-element.47.ou_ref, f32[256,128]{1,0:T(8,128)S(1)} %get-tuple-element.48.ov_ref, f32[256,128]{1,0:T(8,128)S(1)} %get-tuple-element.49.wx_ref, f32[256,128]{1,0:T(8,128)S(1)} %get-tuple-element.50.wy_ref), custom_call_target="tpu_custom_call" | custom-call | flops 4000000 | bytes 4000000 | tf_op jit(solution)/shard_map/inner/pallas_call | solution.py:380
  50.2 1.6 %collective-permute-done.near_ref = f32[384,128]{1,0:T(8,128)S(1)} collective-permute-done((f32[384,128]{1,0:T(8,128)S(1)}, f32[384,128]{1,0:T(8,128)S(1)}, u32[]{:S(2)}, u32[]{:S(2)}) %collective-permute-start) | collective-permute-done | bytes 196640 | tf_op jit(solution)/shard_map/ppermute | solution.py:658
  51.8 0.0 collective-permute-done.1.far_ref
  51.9 1.9 %collective-permute-start.3 = (f32[256,128]{1,0:T(8,128)S(1)}, f32[256,128]{1,0:T(8,128)S(1)}, u32[]{:S(2)}, u32[]{:S(2)}) collective-permute-start(f32[256,128]{1,0:T(8,128)S(1)} %get-tuple-element.61), channel_id=1, source_target_pairs={{0,8},{1,2},{2,1},{3,4},{4,3},{5,6},{6,5},{7,15},{8,0},{9,10},{10,... | collective-permute-start | bytes 393224 | tf_op jit(solution)/shard_map/ppermute | solution.py:657
  53.8 1.8 %collective-permute-start.2 = (f32[256,128]{1,0:T(8,128)S(1)}, f32[256,128]{1,0:T(8,128)S(1)}, u32[]{:S(2)}, u32[]{:S(2)}) collective-permute-start(f32[256,128]{1,0:T(8,128)S(1)} %get-tuple-element.62), channel_id=1, source_target_pairs={{0,1},{1,0},{2,3},{3,2},{4,5},{5,4},{6,7},{7,6},{8,9},{9,8},{10,11... | collective-permute-start | bytes 393224 | tf_op jit(solution)/shard_map/ppermute | solution.py:658
  55.5 4.5 %sides.1 = (f32[2560,128]{1,0:T(8,128)S(1)}, f32[2,224,128]{2,1,0:T(8,128)S(1)}) custom-call(s32[8,128]{1,0:T(8,128)S(4)} %get-tuple-element.32.pos_ref, f32[2048,128]{1,0:T(8,128)S(1)} %get-tuple-element.37.tile_ref, f32[384,128]{1,0:T(8,128)S(1)} %collective-permute-done.near_ref, f32[384,128]{1,0:T(8,128)S(1)} %collective-permute-done.1.far_ref, ...), custom_call_target="tpu_custom_call" | custom-call | flops 5000000 | bytes 5000000 | tf_op jit(solution)/shard_map/sides/pallas_call | solution.py:500
  60.1 0.0 collective-permute-done.3.outer_ref
  60.1 0.0 collective-permute-done.2.inner_ref
  60.1 2.2 %ends.1 = (f32[2560,128]{1,0:T(8,128)S(1)}, f32[2,32,128]{2,1,0:T(8,128)S(1)}) custom-call(s32[8,128]{1,0:T(8,128)S(4)} %get-tuple-element.32.pos_ref, f32[2048,128]{1,0:T(8,128)S(1)} %get-tuple-element.37.tile_ref, f32[384,128]{1,0:T(8,128)S(1)} %collective-permute-done.near_ref, ...), custom_call_target="tpu_custom_call", output_to_operand_aliasing={{0}: (10, {})} | custom-call | tf_op jit(solution)/shard_map/ends/pallas_call | solution.py:577
  62.3 27.1 %all_to_all.11 = f32[256,5,2,128]{3,2,1,0:T(2,128)S(1)} all-to-all(f32[256,5,2,128]{3,2,1,0:T(2,128)S(1)} %bitcast.8), channel_id=1, replica_groups=mesh['gx'=16,'gy'=8] {'gx','gy'}, dimensions={0} | all-to-all | bytes 2621440 | tf_op jit(solution)/shard_map/all_to_all | solution.py:687
  89.4 1.1 %unpack_ice.1 = (f32[112,2,256]{2,1,0:T(2,128)}, f32[3,112,256]{2,1,0:T(8,128)}, f32[2,256,128]{2,1,0:T(8,128)}) custom-call(s32[8,128]{1,0:T(8,128)S(4)} %get-tuple-element.31.starts_ref, f32[2560,128]{1,0:T(8,128)S(1)} %bitcast.9, f32[2,224,128]{2,1,0:T(8,128)S(1)} %get-tuple-element.54.mid_ref, f32[2,32,128]{2,1,0:T(8,128)S(1)} %get-tuple-element.55.end_ref), custom_call_target="tpu_custom_call" | custom-call | tf_op jit(solution)/shard_map/unpack_ice/pallas_call | solution.py:629
  (11 shorter events, 0.1 us)
Async XLA Ops:
  46.2 5.6 %collective-permute-start = (f32[384,128]{1,0:T(8,128)S(1)}, f32[384,128]{1,0:T(8,128)S(1)}, u32[]{:S(2)}, u32[]{:S(2)}) collective-permute-start(f32[384,128]{1,0:T(8,128)S(1)} %get-tuple-element.38), channel_id=1, source_target_pairs={{0,8},{1,9},{2,10},{3,11},{4,12},{5,13},{6,14},{7,15},{8,0},{9,1},... | collective-permute-start | bytes 589832 | tf_op jit(solution)/shard_map/ppermute | solution.py:658
  46.3 5.5 %collective-permute-start.1 = (f32[384,128]{1,0:T(8,128)S(1)}, f32[384,128]{1,0:T(8,128)S(1)}, u32[]{:S(2)}, u32[]{:S(2)}) collective-permute-start(f32[384,128]{1,0:T(8,128)S(1)} %get-tuple-element.39), channel_id=1, source_target_pairs={{0,1},{1,0},{2,3},{3,2},{4,5},{5,4},{6,7},{7,6},{8,16},{9,17},{10,... | collective-permute-start | bytes 589832 | tf_op jit(solution)/shard_map/ppermute | solution.py:657
  51.9 8.2 %collective-permute-start.3 = (f32[256,128]{1,0:T(8,128)S(1)}, f32[256,128]{1,0:T(8,128)S(1)}, u32[]{:S(2)}, u32[]{:S(2)}) collective-permute-start(f32[256,128]{1,0:T(8,128)S(1)} %get-tuple-element.61), channel_id=1, source_target_pairs={{0,8},{1,2},{2,1},{3,4},{4,3},{5,6},{6,5},{7,15},{8,0},{9,10},{10,... | collective-permute-start | bytes 393224 | tf_op jit(solution)/shard_map/ppermute | solution.py:657
  53.8 6.3 %collective-permute-start.2 = (f32[256,128]{1,0:T(8,128)S(1)}, f32[256,128]{1,0:T(8,128)S(1)}, u32[]{:S(2)}, u32[]{:S(2)}) collective-permute-start(f32[256,128]{1,0:T(8,128)S(1)} %get-tuple-element.62), channel_id=1, source_target_pairs={{0,1},{1,0},{2,3},{3,2},{4,5},{5,4},{6,7},{7,6},{8,9},{9,8},{10,11... | collective-permute-start | bytes 393224 | tf_op jit(solution)/shard_map/ppermute | solution.py:658
